TPU v7x, 512 devices: a whole 4x4x16 slice. The times are simulated.
512 devices in a mesh: ctx: 32 (over y_hi, z), tp: 16 (over x, y_lo, core).
Axes of the slice: x: 4, y: 4 (y_hi: 2, y_lo: 2; y = y_hi * 2 + y_lo), z: 16, core: 2. Of those that a mesh axis runs over, the one named last changes fastest.
Arguments:
- queries: bfloat16 [16384, 2048], P('ctx', 'tp'), may hold values from -6 to 6
- keys: bfloat16 [16384, 2048], P('ctx', 'tp'), may hold values from -6 to 6
- values: bfloat16 [16384, 2048], P('ctx', 'tp'), may hold values from -6 to 6
- residual: bfloat16 [16384, 2048], P('ctx', 'tp'), may hold values from -3 to 3
- out_proj: bfloat16 [2048, 2048], P('tp'), may hold values from -0.5 to 0.5
- norm_gain: float32 [2048], replicated, may hold values from 0.1 to 1.9
- in_proj: bfloat16 [2048, 3, 2048], P(None, None, 'tp'), may hold values from -0.125 to 0.125
- feat_taps: float32 [3, 3, 2048], P(None, None, 'tp'), may hold values from -3 to 3
- long_filter: float32 [7, 128], P(None, 'tp'), may hold values from -2 to 2
Outputs:
- hidden: bfloat16 [16384, 2048], P('ctx', 'tp')
- gated: bfloat16 [16384, 2048], P('ctx', 'tp')
All inputs are finite; a program needn't handle non-finite values.
Results may differ from a plain program's by a relative error of at most 0.04.
Values may be sent and summed in bfloat16 or wider, within the bound.
A program may use at most 64 MiB of HBM per device.

v0:
```python
import math

import jax
import jax.numpy as jnp
from jax import lax
from jax.sharding import PartitionSpec as P

HEAD_DIM = 128
GROUP = 16
FEAT_TAPS = 3
FILTER_TAPS = 7
RIM = 8


def padded(cells, sides, width):
    for axis, dim in sides:
        count = lax.axis_size(axis)
        ends = count - 1
        head = lax.slice_in_dim(cells, 0, width, axis=dim)
        tail = lax.slice_in_dim(cells, cells.shape[dim] - width, cells.shape[dim], axis=dim)
        cells = jnp.concatenate(
            [
                lax.ppermute(tail, axis, [(i, (i + 1) % count) for i in range(ends)]),
                cells,
                lax.ppermute(head, axis, [((i + 1) % count, i) for i in range(ends)]),
            ],
            axis=dim,
        )
    return cells


def mirror_place(rows_index, rows_dev, ctx_count):
    half_rows = rows_dev // 2
    device = rows_index // rows_dev
    within = rows_index % rows_dev
    block_idx = jnp.where(within < half_rows, device, 2 * ctx_count - 1 - device)
    return block_idx * half_rows + within % half_rows


def attend_block(running, queries_3d, query_place, key_block, value_block, key_place):
    largest, totals, weighted = running
    scores = jnp.einsum(
        "qhd,khd->hqk", queries_3d, key_block, preferred_element_type=jnp.float32
    ) * HEAD_DIM ** (-0.5)
    visible = (key_place[None, :] <= query_place[:, None])[None]
    scores = jnp.where(visible, scores, -1e30)
    renewed = jnp.maximum(largest, jnp.max(scores, axis=-1))
    weights = jnp.where(visible, jnp.exp(scores - renewed[..., None]), 0.0)
    factor = jnp.exp(largest - renewed)
    totals = totals * factor + jnp.sum(weights, axis=-1)
    weighted = weighted * factor[..., None] + jnp.einsum(
        "hqk,khd->hqd",
        weights.astype(jnp.bfloat16),
        value_block,
        preferred_element_type=jnp.float32,
    )
    return (renewed, totals, weighted)


def local(queries, keys, values, residual, out_proj, norm_gain, in_proj, feat_taps, long_filter):
    rows_dev, head_cols = queries.shape
    heads_here = head_cols // HEAD_DIM
    half_rows = rows_dev // 2
    ctx_count = lax.axis_size("ctx")
    position = lax.axis_index("ctx")
    query_place = mirror_place(
        position * rows_dev + jnp.arange(rows_dev, dtype=jnp.int32), rows_dev, ctx_count
    )
    queries_3d = queries.reshape(rows_dev, heads_here, HEAD_DIM)
    query_halves = (queries_3d[:half_rows], queries_3d[half_rows:])
    place_halves = (query_place[:half_rows], query_place[half_rows:])
    place_tops = (jnp.max(place_halves[0]), jnp.max(place_halves[1]))
    half_state = (
        jnp.full((heads_here, half_rows), -1e30, jnp.float32),
        jnp.zeros((heads_here, half_rows), jnp.float32),
        jnp.zeros((heads_here, half_rows, HEAD_DIM), jnp.float32),
    )
    initial = (half_state, half_state)
    key_piece = lax.all_gather(keys, "ctx", axis=0, tiled=True)
    value_piece = lax.all_gather(values, "ctx", axis=0, tiled=True)
    piece_rows = key_piece.shape[0]
    block_rows = math.gcd(piece_rows, rows_dev)
    sub_rows = math.gcd(block_rows, half_rows)
    sub_count = block_rows // sub_rows
    block_count = piece_rows // block_rows
    key_blocks = key_piece.reshape(block_count, block_rows, heads_here, HEAD_DIM)
    value_blocks = value_piece.reshape(block_count, block_rows, heads_here, HEAD_DIM)
    firsts = 0 + block_rows * jnp.arange(block_count, dtype=jnp.int32)

    def fold_block(state, block_item):
        key_block, value_block, first_row = block_item
        key_place = mirror_place(
            first_row + jnp.arange(block_rows, dtype=jnp.int32), rows_dev, ctx_count
        )
        states = list(state)
        for sub_index in range(sub_count):
            lower = sub_index * sub_rows
            key_sub = key_block[lower : lower + sub_rows]
            value_sub = value_block[lower : lower + sub_rows]
            place_sub = key_place[lower : lower + sub_rows]
            earliest = jnp.min(place_sub)
            for half_index in range(2):

                def compute(
                    current,
                    half_index=half_index,
                    key_sub=key_sub,
                    value_sub=value_sub,
                    place_sub=place_sub,
                ):
                    return attend_block(
                        current,
                        query_halves[half_index],
                        place_halves[half_index],
                        key_sub,
                        value_sub,
                        place_sub,
                    )

                def keep(current):
                    return current

                states[half_index] = lax.cond(
                    earliest <= place_tops[half_index], compute, keep, states[half_index]
                )
        return ((states[0], states[1]), None)

    state, _ = lax.scan(fold_block, initial, (key_blocks, value_blocks, firsts))
    totals = jnp.concatenate([state[0][1], state[1][1]], 1)
    weighted = jnp.concatenate([state[0][2], state[1][2]], 1)
    attended = (
        jnp.transpose(weighted / totals[..., None], (1, 0, 2))
        .reshape(rows_dev, head_cols)
        .astype(jnp.bfloat16)
    )
    own_cols = residual.shape[1]
    head_term = jnp.dot(attended, out_proj, preferred_element_type=jnp.float32)
    summed = lax.psum(head_term.astype(jnp.bfloat16), "tp").astype(jnp.float32)
    full_residual = lax.all_gather(residual, "tp", axis=1, tiled=True)
    gathered = (full_residual.astype(jnp.float32) + summed).astype(jnp.bfloat16)
    hidden = lax.dynamic_slice_in_dim(gathered, lax.axis_index("tp") * own_cols, own_cols, 1)
    widened = gathered.astype(jnp.float32)
    mean_square = jnp.mean(widened * widened, axis=-1, keepdims=True)
    normed = (widened * lax.rsqrt(mean_square + 1e-06) * norm_gain).astype(jnp.bfloat16)
    streams = jnp.dot(
        normed, in_proj.reshape(in_proj.shape[0], 3 * own_cols), preferred_element_type=jnp.float32
    ).astype(jnp.bfloat16)
    first_tail = streams[half_rows - RIM : half_rows]
    second_tail = streams[rows_dev - RIM :]
    rim_rows = padded(jnp.concatenate([second_tail, first_tail], 0), (("ctx", 0),), RIM)
    before_first = rim_rows[:RIM]
    before_second = jnp.where(position == ctx_count - 1, first_tail, rim_rows[3 * RIM :])
    extended = jnp.stack(
        [
            jnp.concatenate([before_first, streams[:half_rows]], 0),
            jnp.concatenate([before_second, streams[half_rows:]], 0),
        ]
    )
    extended = extended.astype(jnp.float32).reshape(2, RIM + half_rows, 3, own_cols)
    span_rows = RIM + half_rows - (FEAT_TAPS - 1)
    featured = jnp.zeros((2, span_rows, 3, own_cols), jnp.float32)
    for tap_index in range(FEAT_TAPS):
        offset = FEAT_TAPS - 1 - tap_index
        featured = (
            featured + feat_taps[tap_index][None, None] * extended[:, offset : offset + span_rows]
        )
    mixture = featured[:, :, 0] * featured[:, :, 2]
    filter_rows = jnp.repeat(long_filter, GROUP, axis=1)
    response = jnp.zeros((2, half_rows, own_cols), jnp.float32)
    for tap_index in range(FILTER_TAPS):
        offset = FILTER_TAPS - 1 - tap_index
        response = (
            response + filter_rows[tap_index][None, None] * mixture[:, offset : offset + half_rows]
        )
    gated_out = (
        (featured[:, FILTER_TAPS - 1 :, 1] * response)
        .astype(jnp.bfloat16)
        .reshape(rows_dev, own_cols)
    )
    return (hidden, gated_out)


def solution(mesh):
    return jax.shard_map(
        local,
        mesh=mesh,
        in_specs=(
            P("ctx", "tp"),
            P("ctx", "tp"),
            P("ctx", "tp"),
            P("ctx", "tp"),
            P("tp", None),
            P(),
            P(None, None, "tp"),
            P(None, None, "tp"),
            P(None, "tp"),
        ),
        out_specs=(P("ctx", "tp"), P("ctx", "tp")),
        check_vma=False,
    )
```

profile of v0, /device:TPU:1, one launch (start us, length us, event | category | flops | bytes accessed | tf_op | source)
XLA Modules:
  0.0 808.3 jit_solution(11345158503666987777)
XLA Ops:
  11.0 161.6 %all-gather.6.cloned.1.call-done = bf16[16384,128]{1,0:T(8,128)(2,1)} async-done(((bf16[512,128]{1,0:T(8,128)(2,1)}), bf16[16384,128]{1,0:T(8,128)(2,1)}) %all-gather.6.cloned.1.call-update) | async-done | bytes 4194320 | tf_op jit(solution)/shard_map/all_gather | solution.py:79
  172.6 161.9 %all-gather.8.cloned.1.call-done = bf16[16384,128]{1,0:T(8,128)(2,1)} async-done(((bf16[512,128]{1,0:T(8,128)(2,1)}), bf16[16384,128]{1,0:T(8,128)(2,1)}) %all-gather.8.cloned.1.call-update) | async-done | bytes 4194320 | tf_op jit(solution)/shard_map/all_gather | solution.py:80
  334.6 308.5 %while.23 = (s32[]{:T(128)}, f32[1,256]{1,0:T(1,128)S(1)}, f32[1,256]{1,0:T(1,128)S(1)}, f32[1,256,128]{2,1,0:T(8,128)S(1)}, f32[1,256]{1,0:T(1,128)S(1)}, /*ind...) while((s32[]{:T(128)}, f32[1,256]{1,0:T(1,128)S(1)}, ...), condition=%wide.region_21.22_spmd, body=%wide.region_2.21_spmd.sunk | while | flops 137646592 | bytes 5601985 | solution.py:128
  344.9 1.0 dynamic-slice_bitcast_fusion.5
  373.8 1.0 dynamic-slice_bitcast_fusion.5
  383.4 1.0 dynamic-slice_bitcast_fusion.5
  393.0 1.0 dynamic-slice_bitcast_fusion.5
  402.6 1.0 dynamic-slice_bitcast_fusion.5
  412.2 1.0 dynamic-slice_bitcast_fusion.5
  421.9 1.0 dynamic-slice_bitcast_fusion.5
  469.9 1.0 dynamic-slice_bitcast_fusion.5
  479.6 1.0 dynamic-slice_bitcast_fusion.5
  489.2 1.0 dynamic-slice_bitcast_fusion.5
  498.8 1.0 dynamic-slice_bitcast_fusion.5
  508.4 1.0 dynamic-slice_bitcast_fusion.5
  518.0 1.0 dynamic-slice_bitcast_fusion.5
  643.1 2.1 convolution_convert_fusion
  645.2 1.6 copy.16
  648.0 138.7 %all-reduce.2.cloned.1.call-done = bf16[512,2048]{1,0:T(8,128)(2,1)} async-done(((bf16[512,2048]{1,0:T(8,128)(2,1)}), bf16[512,2048]{1,0:T(8,128)(2,1)}) %all-reduce.2.cloned.1.call-update) | async-done | bytes 2097168 | tf_op jit(solution)/shard_map/psum | solution.py:138
  786.7 3.2 fusion.57
  789.9 1.3 fusion.64
  791.3 1.3 collective-permute-start.1
  793.3 2.4 collective-permute-done.1
  795.7 3.1 collective-permute-start
  (697 shorter events, 187.4 us)
Async XLA Ops:
  7.2 635.9 %copy-start = (bf16[128,2048]{1,0:T(8,128)(2,1)S(1)}, bf16[128,2048]{1,0:T(8,128)(2,1)}, u32[]{:S(2)}) copy-start(bf16[128,2048]{1,0:T(8,128)(2,1)} %param.23) | copy-start | bytes 1572868
  7.2 165.4 %all-gather.6.cloned.1.call-start = ((), (), s32[]{:S(2)}) async-start(), calls=%async_computation.1 | async-start | bytes 4325376 | tf_op jit(solution)/shard_map/all_gather | solution.py:79
  7.9 326.6 %all-gather.8.cloned.1.call-start = ((), (), s32[]{:S(2)}) async-start(), calls=%async_computation.2 | async-start | bytes 4325376 | tf_op jit(solution)/shard_map/all_gather | solution.py:80
  8.7 639.3 %all-gather.4.cloned.1.call-start = ((), (), s32[]{:S(2)}) async-start(), calls=%async_computation | async-start | bytes 2228224 | tf_op jit(solution)/shard_map/all_gather | solution.py:139
  9.4 777.3 %all-reduce.2.cloned.1.call-start = ((), (), s32[]{:S(2)}) async-start(), calls=%async_computation.3 | async-start | bytes 4194304 | tf_op jit(solution)/shard_map/psum | solution.py:138
  643.1 2.1 copy-start.1
  645.2 1.6 copy-start.4
  645.2 2.7 copy-start.3
  647.9 142.0 %copy-start.2 = (bf16[2048,3,128]{0,2,1:T(8,128)(2,1)S(1)}, bf16[2048,3,128]{0,2,1:T(8,128)(2,1)}, u32[]{:S(2)}) copy-start(bf16[2048,3,128]{0,2,1:T(8,128)(2,1)} %copy.16) | copy-start | bytes 4718596
  647.9 142.0 %copy-start.5 = (f32[2048]{0:T(1024)S(1)}, f32[2048]{0:T(1024)}, u32[]{:S(2)}) copy-start(f32[2048]{0:T(1024)} %param.24) | copy-start | bytes 24580
  791.3 4.4 collective-permute-start.1
  795.7 3.9 collective-permute-start
Sparse Core Ops, SparseCore 0:
  11.1 161.3 all-gather.5
  175.7 158.7 all-gather.7
  336.6 48.2 all-gather.3
  645.3 141.3 all-reduce.1
where the time goes:
time: 821 us; the launch traced here: 808 us
  waiting for transfers between devices  467 us (57%)
  loops' own time  166 us (20%)
  other arithmetic  60.6 us (7%)
  local copies, waits for them, and re-layouts  57.1 us (7%)
  matrix products  39.2 us (5%)
  between operations  14.1 us (2%)
    another operation x1, loops' own time, local(): state, _ = lax.scan(fold_block, initial, (key_blocks, value_blocks, firsts))  163 us
    all_gather x1, waiting for transfers between devices, local(): value_piece = lax.all_gather(values, 'ctx', axis=0, tiled=True)  162 us
    all_gather x1, waiting for transfers between devices, local(): key_piece = lax.all_gather(keys, 'ctx', axis=0, tiled=True)  162 us
    psum x1, waiting for transfers between devices, local(): summed = lax.psum(head_term.astype(jnp.bfloat16), 'tp').astype(jnp.float32)  139 us
    slice x32, local copies, waits for them, and re-layouts, fold_block(): value_sub = value_block[lower:lower + sub_rows]  30.8 us
    reduce_min x32, other arithmetic, fold_block(): earliest = jnp.min(place_sub)  22.9 us
    add x33, other arithmetic, mirror_place(): return block_idx * half_rows + within % half_rows  22.5 us
    dot_general x65, matrix products, attend_block(): jnp.einsum('hqk,khd->hqd', weights.astype(jnp.bfloat16), value_block, pre...  21.5 us
  transfers between devices with their start and end apart: 6, of which 5 were waited for; matrix products, arithmetic and copies ran while one was open for 19% of the time, Pallas kernels for 0%

commit v1 on v0

v1 whole, which is shorter than its diff:
```python
import functools

import jax
import jax.numpy as jnp
from jax import lax
from jax.experimental import pallas as pl
from jax.experimental.pallas import tpu as pltpu
from jax.sharding import PartitionSpec as P

MESH = pl.DeviceIdType.MESH
LANES = 128
GROUP = 16
FEAT_TAPS = 3
FILTER_TAPS = 7
RIM = 8
LOW = -1e30
LOG2E = 1.4426950408889634
F32 = jnp.float32
BF16 = jnp.bfloat16


def kernel(
    ring,
    q_ref,
    k_ref,
    v_ref,
    res_ref,
    outp_ref,
    gain_ref,
    inp_ref,
    taps_ref,
    filt_ref,
    hid_ref,
    gated_ref,
    kbuf,
    vbuf,
    qpar,
    acc_own,
    acc_par,
    max_own,
    max_par,
    o_send,
    o_recv,
    st_send,
    st_recv,
    wout,
    win,
    att_all,
    hid_all,
    hid_acc,
    str_acc,
    sq_acc,
    str_ref,
    halo,
    ext,
    mix,
    in_sem,
    ks_sem,
    kr_sem,
    vs_sem,
    vr_sem,
    x_send,
    x_recv,
    w_send,
    w_recv,
    g_send,
    g_recv,
):
    rows, width = q_ref.shape
    half = rows // 2
    top = ring // 2
    n_ctx = 2 * ring
    n_tp = wout.shape[0]
    n_x = n_tp // 4
    dev = lax.axis_index("ctx")
    y_hi = dev // ring
    z = lax.rem(dev, ring)
    tp = lax.axis_index("tp")
    x = tp // 4
    y_lo = lax.rem(tp, 4) // 2
    core = lax.rem(tp, 2)
    scale = LOG2E * width**-0.5

    def ctx_id(y_at, z_at):
        return {"ctx": y_at * ring + z_at}

    right = ctx_id(y_hi, lax.rem(z + 1, ring))
    left = ctx_id(y_hi, lax.rem(z + ring - 1, ring))
    across = ctx_id(1 - y_hi, z)
    after = {"ctx": lax.rem(dev + 1, n_ctx)}
    before = {"ctx": lax.rem(dev + n_ctx - 1, n_ctx)}

    def tp_at(dx, dy, dc):
        return (
            lax.rem(x + dx + n_x, n_x) * 4
            + (1 - y_lo if dy else y_lo) * 2
            + (1 - core if dc else core)
        )

    barrier = pltpu.get_barrier_semaphore()
    for other in (right, left, across, after, before):
        pl.semaphore_signal(barrier, inc=1, device_id=other, device_id_type=MESH)

    def greet(step, carry):
        peer = lax.rem(tp + step, n_tp)
        pl.semaphore_signal(barrier, inc=1, device_id={"tp": peer}, device_id_type=MESH)
        return carry

    lax.fori_loop(1, n_tp, greet, 0)

    loads = [
        pltpu.make_async_copy(
            inp_ref.at[s], win.at[:, s * LANES : (s + 1) * LANES], in_sem.at[s]
        )
        for s in range(3)
    ]
    for load in loads:
        load.start()
    pl.semaphore_wait(barrier, n_tp - 1 + 5)

    def remote(src, dst, send, recv, to):
        return pltpu.make_async_remote_copy(
            src_ref=src, dst_ref=dst, send_sem=send, recv_sem=recv, device_id=to, device_id_type=MESH
        )

    def key_copy(src, slot, to):
        return remote(src, kbuf.at[slot], ks_sem.at[slot], kr_sem.at[slot], to)

    def value_copy(src, slot, to):
        return remote(src, vbuf.at[slot], vs_sem.at[slot], vr_sem.at[slot], to)

    key_copy(k_ref, 1, right).start()
    key_copy(k_ref, ring - 1, left).start()
    q_copy = remote(q_ref, qpar, x_send.at[0], x_recv.at[0], across)
    q_copy.start()
    value_copy(v_ref, 1, right).start()
    value_copy(v_ref, ring - 1, left).start()

    def out_copy(step):
        peer = lax.rem(tp + step, n_tp)
        cols = pl.ds(pl.multiple_of(peer * LANES, LANES), LANES)
        return remote(
            outp_ref.at[:, cols], wout.at[tp], w_send.at[step], w_recv.at[step], {"tp": peer}
        )

    def out_start(step, carry):
        out_copy(step).start()
        return carry

    lax.fori_loop(1, n_tp, out_start, 0)
    wout[tp] = outp_ref[:, pl.ds(pl.multiple_of(tp * LANES, LANES), LANES)]

    for acc, top_ref in ((acc_own, max_own), (acc_par, max_par)):
        acc[...] = jnp.zeros_like(acc)
        top_ref[...] = jnp.full(top_ref.shape, LOW, F32)

    ones = jnp.ones((half, LANES), BF16)
    tri = lax.broadcasted_iota(jnp.int32, (half, half), 0) >= lax.broadcasted_iota(
        jnp.int32, (half, half), 1
    )

    def unit(queries, acc, top_ref, offset, keys, values, masked=False):
        at = pl.ds(offset, half)
        scores = lax.dot_general(
            queries[at, :], keys, (((1,), (1,)), ((), ())), preferred_element_type=F32
        )
        if masked:
            scores = jnp.where(tri, scores, LOW)
        old = top_ref[at, :]
        new = jnp.maximum(old, jnp.max(scores, axis=1, keepdims=True))
        top_ref[at, :] = new
        wide = jnp.concatenate([new] * (half // LANES), axis=1)
        weights = jnp.exp2((scores - wide) * scale).astype(BF16)
        factor = jnp.exp2((old - new) * scale)
        acc[at, :] = acc[at, :] * jnp.concatenate([factor, factor], axis=1) + jnp.dot(
            weights, jnp.concatenate([values, ones], axis=1), preferred_element_type=F32
        )

    row_c = pl.multiple_of(y_hi * half, half)

    def partner_units(keys, values):
        unit(qpar, acc_par, max_par, half, keys[:half, :], values[:half, :])
        at = pl.ds(row_c, half)
        unit(qpar, acc_par, max_par, row_c, keys[at, :], values[at, :])

    def own_units(keys, values, slot):
        unit(q_ref, acc_own, max_own, half, keys[:half, :], values[:half, :])
        row_d = pl.multiple_of(jnp.where(slot <= z, 0, half), half)
        at = pl.ds(row_d, half)
        unit(q_ref, acc_own, max_own, row_d, keys[at, :], values[at, :])

    unit(q_ref, acc_own, max_own, 0, k_ref[:half, :], v_ref[:half, :], True)
    unit(q_ref, acc_own, max_own, half, k_ref[half:, :], v_ref[half:, :], True)
    unit(q_ref, acc_own, max_own, half, k_ref[:half, :], v_ref[:half, :])
    q_copy.wait_recv()
    partner_units(k_ref, v_ref)

    def turn(step, carry):
        back = ring - step
        key_copy(k_ref, step, right).wait_recv()
        key_copy(kbuf.at[step], step + 1, right).start()
        key_copy(k_ref, back, left).wait_recv()

        @pl.when(step < top - 1)
        def _():
            key_copy(kbuf.at[back], back - 1, left).start()

        value_copy(v_ref, step, right).wait_recv()

        @pl.when(step < top - 1)
        def _():
            value_copy(vbuf.at[step], step + 1, right).start()

        value_copy(v_ref, back, left).wait_recv()
        value_copy(vbuf.at[back], back - 1, left).start()
        for slot in (step, back):
            partner_units(kbuf.at[slot], vbuf.at[slot])
            own_units(kbuf.at[slot], vbuf.at[slot], slot)
        return carry

    lax.fori_loop(1, top, turn, 0)
    key_copy(k_ref, top, right).wait_recv()
    value_copy(v_ref, top, left).wait_recv()
    partner_units(kbuf.at[top], vbuf.at[top])

    def settle(acc, top_ref):
        total = acc[:, LANES:]
        seen = total > 0.0
        inverse = 1.0 / jnp.where(seen, total, 1.0)
        level = jnp.where(seen, top_ref[...] * scale + jnp.log2(jnp.where(seen, total, 1.0)), LOW)
        return acc[:, :LANES] * inverse, level

    diagonal = lax.broadcasted_iota(jnp.int32, (LANES, LANES), 0) == lax.broadcasted_iota(
        jnp.int32, (LANES, LANES), 1
    )
    mean_par, level_par = settle(acc_par, max_par)
    o_send[...] = mean_par.astype(BF16)
    st_send[...] = jnp.zeros_like(st_send)
    for g in range(rows // LANES):
        block = level_par[g * LANES : (g + 1) * LANES, :]
        st_send[g : g + 1, :] = jnp.sum(jnp.where(diagonal, block, 0.0), axis=0, keepdims=True)
    o_copy = remote(o_send, o_recv, x_send.at[1], x_recv.at[1], across)
    st_copy = remote(st_send, st_recv, x_send.at[2], x_recv.at[2], across)
    st_copy.start()
    o_copy.start()
    own_units(kbuf.at[top], vbuf.at[top], top)
    mean_own, level_own = settle(acc_own, max_own)
    for load in loads:
        load.wait()
    st_copy.wait_recv()
    o_copy.wait_recv()
    for g in range(rows // LANES):
        at = slice(g * LANES, (g + 1) * LANES)
        line = jnp.broadcast_to(st_recv[g : g + 1, :], (LANES, LANES))
        level_other = jnp.sum(jnp.where(diagonal, line, 0.0), axis=1, keepdims=True)
        here = level_own[at, :]
        most = jnp.maximum(here, level_other)
        w_own = jnp.exp2(here - most)
        w_other = jnp.exp2(level_other - most)
        joined = (w_own * mean_own[at, :] + w_other * o_recv[at, :].astype(F32)) / (w_own + w_other)
        att_all[tp, at, :] = joined.astype(BF16)

    mid = rows // 2
    whole, head, tail = pl.ds(0, rows), pl.ds(0, mid), pl.ds(mid, mid)
    MOVES = [
        ((0, 0), whole, "y"),
        ((0, 0), whole, "xp"),
        ((0, 0), whole, "xm"),
        ((0, 0), whole, "c"),
        ((0, 1), whole, "xp"),
        ((0, 1), whole, "xm"),
        ((0, 1), whole, "c"),
        ((-1, 0), head, "xp"),
        ((-1, 0), whole, "c"),
        ((1, 0), tail, "xm"),
        ((1, 0), whole, "c"),
        ((-1, 1), head, "xp"),
        ((-1, 1), whole, "c"),
        ((1, 1), tail, "xm"),
        ((1, 1), whole, "c"),
        ((2, 0), whole, "c"),
        ((2, 1), whole, "c"),
    ]
    targets = {
        "y": {"tp": tp_at(0, 1, 0)},
        "xp": {"tp": tp_at(1, 0, 0)},
        "xm": {"tp": tp_at(-1, 0, 0)},
        "c": {"tp": tp_at(0, 0, 1)},
    }

    def gather(which, buf, consume):
        def move(n):
            (dx, dy), part, to = MOVES[n]
            chunk = tp_at(dx, dy, 0)
            ref = buf.at[chunk, part, :]
            return remote(ref, ref, g_send.at[which, n], g_recv.at[which, n], targets[to])

        def arrive(n):
            (dx, dy), part, to = MOVES[n]
            sx = dx + {"xp": -1, "xm": 1}.get(to, 0)
            sy = 1 - dy if to == "y" else dy
            chunk = tp_at(sx, sy, 1 if to == "c" else 0)
            ref = buf.at[chunk, part, :]
            remote(ref, ref, g_send.at[which, n], g_recv.at[which, n], targets[to]).wait_recv()

        def go(*moves):
            for n in moves:
                move(n).start()

        def pair(dx, dy):
            consume(tp_at(dx, dy, 0) // 2)

        go(0, 1, 2, 3)
        arrive(3)
        pair(0, 0)
        arrive(0)
        go(4, 5, 6)
        arrive(1)
        go(7, 8)
        arrive(2)
        go(9, 10)
        arrive(6)
        pair(0, 1)
        arrive(4)
        go(11, 12)
        arrive(5)
        go(13, 14)
        arrive(8)
        pair(-1, 0)
        arrive(10)
        pair(1, 0)
        arrive(7)
        arrive(9)
        go(15)
        arrive(12)
        pair(-1, 1)
        arrive(14)
        pair(1, 1)
        arrive(11)
        arrive(13)
        go(16)
        arrive(15)
        pair(2, 0)
        arrive(16)
        pair(2, 1)
        return [move(n) for n in range(len(MOVES))]

    def out_arrive(step, carry):
        out_copy(step).wait_recv()
        return carry

    lax.fori_loop(1, n_tp, out_arrive, 0)
    hid_acc[...] = res_ref[...].astype(F32)

    def project_out(chip):
        left_side = jnp.concatenate([att_all[2 * chip], att_all[2 * chip + 1]], axis=1)
        weight = jnp.concatenate([wout[2 * chip], wout[2 * chip + 1]], axis=0)
        hid_acc[...] += jnp.dot(left_side, weight, preferred_element_type=F32)

    moves = gather(0, att_all, project_out)
    hidden = hid_acc[...].astype(BF16)
    hid_all[tp] = hidden
    hid_ref[...] = hidden
    str_acc[...] = jnp.zeros_like(str_acc)
    sq_acc[...] = jnp.zeros_like(sq_acc)

    def project_in(chip):
        sides = []
        for c in range(2):
            wide = hid_all[2 * chip + c].astype(F32)
            sq_acc[...] += wide * wide
            sides.append((wide * gain_ref[pl.ds(2 * chip + c, 1), :]).astype(BF16))
        at = pl.ds(pl.multiple_of(chip * 2 * LANES, 2 * LANES), 2 * LANES)
        str_acc[...] += jnp.dot(
            jnp.concatenate(sides, axis=1), win[at, :], preferred_element_type=F32
        )

    moves += gather(1, hid_all, project_in)
    mean_square = jnp.sum(sq_acc[...], axis=1, keepdims=True) / (n_tp * LANES)
    streams = (str_acc[...] * lax.rsqrt(mean_square + 1e-6)).astype(BF16)
    str_ref[...] = streams
    edge = 2 * RIM
    rim_copies = [
        remote(str_ref.at[half - edge : half, :], halo.at[0], x_send.at[3], x_recv.at[3], after),
        remote(str_ref.at[rows - edge : rows, :], halo.at[1], x_send.at[4], x_recv.at[4], before),
    ]
    for copy in rim_copies:
        copy.start()
    spread = streams.astype(F32)
    ext[0, RIM:, :] = spread[:half]
    ext[1, RIM:, :] = spread[half:]
    lane_group = lax.broadcasted_iota(jnp.int32, (FILTER_TAPS, LANES), 1) // GROUP
    filt = jnp.zeros((FILTER_TAPS, LANES), F32)
    for g in range(LANES // GROUP):
        filt = jnp.where(lane_group == g, filt_ref[:, g : g + 1], filt)
    for copy in rim_copies:
        copy.wait_recv()
    first_tail = str_ref[half - edge : half, :].astype(F32)[RIM:]
    ext[0, :RIM, :] = jnp.where(dev == 0, 0.0, halo[0].astype(F32)[RIM:])
    ext[1, :RIM, :] = jnp.where(dev == n_ctx - 1, first_tail, halo[1].astype(F32)[RIM:])
    span = half + FILTER_TAPS - 1
    for side in range(2):

        def featured(stream, start, count, side=side):
            cols = slice(stream * LANES, (stream + 1) * LANES)
            total = None
            for j in range(FEAT_TAPS):
                low = start + FEAT_TAPS - 1 - j
                term = taps_ref[j, stream : stream + 1, :] * ext[side, low : low + count, cols]
                total = term if total is None else total + term
            return total

        mix[0:span, :] = featured(0, 0, span) * featured(2, 0, span)
        response = None
        for j in range(FILTER_TAPS):
            low = FILTER_TAPS - 1 - j
            term = filt[j : j + 1, :] * mix[low : low + half, :]
            response = term if response is None else response + term
        out = featured(1, FILTER_TAPS - 1, half) * response
        gated_ref[side * half : (side + 1) * half, :] = out.astype(BF16)

    def drain(slot, carry):
        key_copy(k_ref, slot, right).wait_send()
        value_copy(v_ref, slot, right).wait_send()
        return carry

    lax.fori_loop(1, ring, drain, 0)

    def out_drain(step, carry):
        out_copy(step).wait_send()
        return carry

    lax.fori_loop(1, n_tp, out_drain, 0)
    for copy in [q_copy, st_copy, o_copy] + rim_copies + moves:
        copy.wait_send()


def local(queries, keys, values, residual, out_proj, norm_gain, in_proj, feat_taps, long_filter):
    rows, width = queries.shape
    half = rows // 2
    n_tp = lax.axis_size("tp")
    ring = lax.axis_size("ctx") // 2
    vmem = pl.BlockSpec(memory_space=pltpu.VMEM)
    anywhere = pl.BlockSpec(memory_space=pl.ANY)
    dma = pltpu.SemaphoreType.DMA
    shape = jax.ShapeDtypeStruct((rows, width), BF16)
    return pl.pallas_call(
        functools.partial(kernel, ring),
        out_shape=(shape, shape),
        in_specs=[vmem] * 6 + [anywhere] + [vmem] * 2,
        out_specs=(vmem, vmem),
        scratch_shapes=[
            pltpu.VMEM((ring, rows, width), BF16),
            pltpu.VMEM((ring, rows, width), BF16),
            pltpu.VMEM((rows, width), BF16),
            pltpu.VMEM((rows, 2 * width), F32),
            pltpu.VMEM((rows, 2 * width), F32),
            pltpu.VMEM((rows, width), F32),
            pltpu.VMEM((rows, width), F32),
            pltpu.VMEM((rows, width), BF16),
            pltpu.VMEM((rows, width), BF16),
            pltpu.VMEM((8, LANES), F32),
            pltpu.VMEM((8, LANES), F32),
            pltpu.VMEM((n_tp, LANES, LANES), BF16),
            pltpu.VMEM((n_tp * LANES, 3 * LANES), BF16),
            pltpu.VMEM((n_tp, rows, width), BF16),
            pltpu.VMEM((n_tp, rows, width), BF16),
            pltpu.VMEM((rows, LANES), F32),
            pltpu.VMEM((rows, 3 * LANES), F32),
            pltpu.VMEM((rows, LANES), F32),
            pltpu.VMEM((rows, 3 * LANES), BF16),
            pltpu.VMEM((2, 2 * RIM, 3 * LANES), BF16),
            pltpu.VMEM((2, RIM + half, 3 * LANES), F32),
            pltpu.VMEM((RIM + half, LANES), F32),
            dma((3,)),
            dma((ring,)),
            dma((ring,)),
            dma((ring,)),
            dma((ring,)),
            dma((5,)),
            dma((5,)),
            dma((n_tp,)),
            dma((n_tp,)),
            dma((2, 17)),
            dma((2, 17)),
        ],
        compiler_params=pltpu.CompilerParams(
            collective_id=0, has_side_effects=True, vmem_limit_bytes=48 * 1024 * 1024
        ),
        cost_estimate=pl.CostEstimate(
            flops=4 * 10**9, bytes_accessed=4 * 10**6, transcendentals=5 * 10**6
        ),
    )(
        queries,
        keys,
        values,
        residual,
        out_proj,
        norm_gain.reshape(n_tp, LANES),
        jnp.transpose(in_proj, (1, 0, 2)),
        feat_taps,
        long_filter,
    )


def solution(mesh):
    return jax.shard_map(
        local,
        mesh=mesh,
        in_specs=(
            P("ctx", "tp"),
            P("ctx", "tp"),
            P("ctx", "tp"),
            P("ctx", "tp"),
            P("tp", None),
            P(),
            P(None, None, "tp"),
            P(None, None, "tp"),
            P(None, "tp"),
        ),
        out_specs=(P("ctx", "tp"), P("ctx", "tp")),
        check_vma=False,
    )
```

time: 821 us -> 118 us (0.14); the launches traced: 808 us -> 117 us
  waiting for transfers between devices: 467 us -> 0 us
  loops' own time: 166 us -> 0 us
  Pallas kernels: 0 us -> 107 us
  other arithmetic: 60.6 us -> 0 us
  local copies, waits for them, and re-layouts: 57.1 us -> 9.44 us
  matrix products: 39.2 us -> 0 us
  between operations: 14.1 us -> 0.66 us
    all_gather x3 -> x0, waiting for transfers between devices: 324 us -> none  [the longest x1 162 us: local(): value_piece = lax.all_gather(values, 'ctx', axis=0, tiled=True)]
    another operation x129 -> x0, loops' own time: 166 us -> none  [the longest x1 163 us: local(): state, _ = lax.scan(fold_block, initial, (key_blocks, value_blocks, firsts))]
    psum x1 -> x0, waiting for transfers between devices: 139 us -> none  [local(): summed = lax.psum(head_term.astype(jnp.bfloat16), 'tp').astype(jnp.float32)]
    pallas_call x0 -> x1, Pallas kernels: none -> 107 us  [local(): pl.pallas_call(functools.partial(kernel, ring), out_shape=(shape, shape),...]
    dot_general x132 -> x0, matrix products: 39.2 us -> none  [the longest x65 21.5 us: attend_block(): jnp.einsum('hqk,khd->hqd', weights.astype(jnp.bfloat16), value_block, pre...]
    slice x37 -> x0, local copies, waits for them, and re-layouts: 32 us -> none  [the longest x32 30.8 us: fold_block(): value_sub = value_block[lower:lower + sub_rows]]
    add x99 -> x0, other arithmetic: 23.9 us -> none  [the longest x33 22.5 us: mirror_place(): return block_idx * half_rows + within % half_rows]
    reduce_min x32 -> x0, other arithmetic: 22.9 us -> none  [fold_block(): earliest = jnp.min(place_sub)]
  transfers between devices with their start and end apart: 6 -> 0, of which waited for: 5 -> 0; matrix products, arithmetic and copies ran while one was open for 19% -> 0% of each run, Pallas kernels for 0% -> 0%
where the time goes in v1:
time: 118 us; the launch traced here: 117 us
  Pallas kernels  107 us (91%)
  local copies, waits for them, and re-layouts  9.44 us (8%)
    pallas_call x1, Pallas kernels, local(): pl.pallas_call(functools.partial(kernel, ring), out_shape=(shape, shape),...  107 us
    unnamed x20, local copies, waits for them, and re-layouts  9.44 us

profile of v1, /device:TPU:1, one launch (start us, length us, event | category | flops | bytes accessed | tf_op | source)
XLA Modules:
  0.0 117.3 jit_solution(4409115066874680633)
XLA Ops:
  0.6 0.0 copy-start
  0.6 1.4 %copy-done = bf16[2048,3,128]{2,0,1:T(8,128)(2,1)S(1)} copy-done((bf16[2048,3,128]{2,0,1:T(8,128)(2,1)S(1)}, bf16[2048,3,128]{2,0,1:T(8,128)(2,1)}, u32[]{:S(2)}) %copy-start) | copy-done | bytes 1572888
  2.0 0.0 copy-start.1
  2.0 1.0 copy-done.1
  3.1 0.0 copy-start.2
  3.1 0.9 copy-done.2
  4.0 0.0 copy-start.3
  4.0 0.9 copy-done.3
  4.9 0.0 copy-start.4
  4.9 0.9 copy-done.4
  5.8 0.0 copy-start.5
  5.8 0.9 copy-done.5
  6.7 0.0 copy-start.6
  6.7 0.7 copy-done.6
  7.4 0.0 copy-start.7
  7.4 0.7 copy-done.7
  8.1 0.0 copy-start.8
  8.1 0.7 copy-done.8
  8.8 107.2 %shard_map.104 = (bf16[512,128]{1,0:T(8,128)(2,1)S(1)}, bf16[512,128]{1,0:T(8,128)(2,1)S(1)}) custom-call(bf16[512,128]{1,0:T(8,128)(2,1)S(1)} %copy-done.2, bf16[512,128]{1,0:T(8,128)(2,1)S(1)} %copy-done.3, bf16[512,128]{1,0:T(8,128)(2,1)S(1)} %copy-done.4, bf16[512,128]{1,0:T(8,128)(2,1)S(1)} %copy-done.5, bf16[128,2048]{1,0:T(8,128)(2,1)S(1)} %copy-done.1, ...), custom_call_target="tpu_custom_call" | custom-call | flops 4000000000 | bytes 4000000 | tf_op jit(solution)/shard_map/pallas_call | solution.py:447
  116.0 0.7 copy.13
  116.6 0.7 copy.14
Async XLA Ops:
  0.6 1.4 %copy-start = (bf16[2048,3,128]{2,0,1:T(8,128)(2,1)S(1)}, bf16[2048,3,128]{2,0,1:T(8,128)(2,1)}, u32[]{:S(2)}) copy-start(bf16[2048,3,128]{2,0,1:T(8,128)(2,1)} %param.15) | copy-start | bytes 4718596
  2.0 1.0 copy-start.1
  3.1 0.9 copy-start.2
  4.0 0.9 copy-start.3
  4.9 0.9 copy-start.4
  5.8 0.9 copy-start.5
  6.7 0.7 copy-start.6
  7.4 0.7 copy-start.7
  8.1 0.7 copy-start.8

commit v2 on v1

v2 whole, which is shorter than its diff:
```python
import functools

import jax
import jax.numpy as jnp
from jax import lax
from jax.experimental import pallas as pl
from jax.experimental.pallas import tpu as pltpu
from jax.sharding import PartitionSpec as P

MESH = pl.DeviceIdType.MESH
LANES = 128
GROUP = 16
FEAT_TAPS = 3
FILTER_TAPS = 7
RIM = 8
LOW = -1e30
LOG2E = 1.4426950408889634
F32 = jnp.float32
BF16 = jnp.bfloat16


def kernel(
    ring,
    q_hbm,
    k_hbm,
    v_hbm,
    res_hbm,
    outp_hbm,
    gain_hbm,
    inp_hbm,
    taps_hbm,
    filt_hbm,
    hid_ref,
    gated_ref,
    q_ref,
    k_ref,
    v_ref,
    res_ref,
    gain_ref,
    taps_ref,
    filt_ref,
    kbuf,
    vbuf,
    qpar,
    acc_own,
    acc_par,
    max_own,
    max_par,
    o_send,
    o_recv,
    st_send,
    st_recv,
    wout,
    win,
    att_all,
    hid_all,
    hid_acc,
    str_acc,
    sq_acc,
    str_ref,
    halo,
    ext,
    mix,
    in_sem,
    ks_sem,
    kr_sem,
    vs_sem,
    vr_sem,
    x_send,
    x_recv,
    w_send,
    w_recv,
    g_send,
    g_recv,
):
    rows, width = q_ref.shape
    half = rows // 2
    quarter = half // 2
    top = ring // 2
    n_ctx = 2 * ring
    n_tp = wout.shape[0]
    n_x = n_tp // 4
    dev = lax.axis_index("ctx")
    y_hi = dev // ring
    z = lax.rem(dev, ring)
    tp = lax.axis_index("tp")
    x = tp // 4
    y_lo = lax.rem(tp, 4) // 2
    core = lax.rem(tp, 2)
    scale = LOG2E * width**-0.5

    def ctx_id(y_at, z_at):
        return {"ctx": y_at * ring + z_at}

    right = ctx_id(y_hi, lax.rem(z + 1, ring))
    left = ctx_id(y_hi, lax.rem(z + ring - 1, ring))
    across = ctx_id(1 - y_hi, z)
    after = {"ctx": lax.rem(dev + 1, n_ctx)}
    before = {"ctx": lax.rem(dev + n_ctx - 1, n_ctx)}

    def tp_at(dx, dy, dc):
        return (
            lax.rem(x + dx + n_x, n_x) * 4
            + (1 - y_lo if dy else y_lo) * 2
            + (1 - core if dc else core)
        )

    barrier = pltpu.get_barrier_semaphore()
    for other in (right, left, across, after, before):
        pl.semaphore_signal(barrier, inc=1, device_id=other, device_id_type=MESH)

    def greet(step, carry):
        peer = lax.rem(tp + step, n_tp)
        pl.semaphore_signal(barrier, inc=1, device_id={"tp": peer}, device_id_type=MESH)
        return carry

    lax.fori_loop(1, n_tp, greet, 0)

    own_cols = pl.ds(pl.multiple_of(tp * LANES, LANES), LANES)
    loads = []
    for src, dst in [
        (q_hbm, q_ref),
        (k_hbm, k_ref),
        (v_hbm, v_ref),
        (res_hbm, res_ref),
        (gain_hbm, gain_ref),
        (taps_hbm, taps_ref),
        (filt_hbm, filt_ref),
        (outp_hbm.at[:, own_cols], wout.at[tp]),
    ] + [(inp_hbm.at[s], win.at[:, s * LANES : (s + 1) * LANES]) for s in range(3)]:
        load = pltpu.make_async_copy(src, dst, in_sem.at[len(loads)])
        load.start()
        loads.append(load)

    for acc, top_ref in ((acc_own, max_own), (acc_par, max_par)):
        acc[...] = jnp.zeros_like(acc)
        top_ref[...] = jnp.full(top_ref.shape, LOW, F32)
    pl.semaphore_wait(barrier, n_tp - 1 + 5)

    def remote(src, dst, send, recv, to):
        return pltpu.make_async_remote_copy(
            src_ref=src, dst_ref=dst, send_sem=send, recv_sem=recv, device_id=to, device_id_type=MESH
        )

    def key_copy(src, slot, to):
        return remote(src, kbuf.at[slot], ks_sem.at[slot], kr_sem.at[slot], to)

    def value_copy(src, slot, to):
        return remote(src, vbuf.at[slot], vs_sem.at[slot], vr_sem.at[slot], to)

    key_copy(k_hbm, 1, right).start()
    key_copy(k_hbm, ring - 1, left).start()
    q_copy = remote(q_hbm, qpar, x_send.at[0], x_recv.at[0], across)
    q_copy.start()
    value_copy(v_hbm, 1, right).start()
    value_copy(v_hbm, ring - 1, left).start()

    def out_copy(step):
        peer = lax.rem(tp + step, n_tp)
        cols = pl.ds(pl.multiple_of(peer * LANES, LANES), LANES)
        return remote(
            outp_hbm.at[:, cols], wout.at[tp], w_send.at[step], w_recv.at[step], {"tp": peer}
        )

    def out_start(step, carry):
        out_copy(step).start()
        return carry

    ones = jnp.ones((half, LANES), BF16)
    tri = lax.broadcasted_iota(jnp.int32, (half, half), 0) >= lax.broadcasted_iota(
        jnp.int32, (half, half), 1
    )

    def unit(queries, acc, top_ref, offset, blocks, masked=False):
        at = pl.ds(offset, half)
        rows_q = queries[at, :]
        scores = [
            lax.dot_general(rows_q, keys, (((1,), (1,)), ((), ())), preferred_element_type=F32)
            for keys, _ in blocks
        ]
        if masked:
            scores = [jnp.where(tri, block, LOW) for block in scores]
        old = top_ref[at, :]
        best = functools.reduce(jnp.maximum, scores)
        new = jnp.maximum(old, jnp.max(best, axis=1, keepdims=True))
        top_ref[at, :] = new
        wide = jnp.concatenate([new] * (half // LANES), axis=1)
        factor = jnp.exp2((old - new) * scale)
        total = acc[at, :] * jnp.concatenate([factor, factor], axis=1)
        for block, (_, values) in zip(scores, blocks):
            weights = jnp.exp2((block - wide) * scale).astype(BF16)
            total = total + jnp.dot(
                weights, jnp.concatenate([values, ones], axis=1), preferred_element_type=F32
            )
        acc[at, :] = total

    row_c = pl.multiple_of(y_hi * half, half)

    def first_units(pairs):
        blocks = [(keys[:half, :], values[:half, :]) for keys, values in pairs]
        unit(qpar, acc_par, max_par, half, blocks)
        return blocks

    def third_unit(pairs):
        at = pl.ds(row_c, half)
        unit(qpar, acc_par, max_par, row_c, [(keys[at, :], values[at, :]) for keys, values in pairs])

    def last_unit(keys, values, slot):
        row_d = pl.multiple_of(jnp.where(slot <= z, 0, half), half)
        at = pl.ds(row_d, half)
        unit(q_ref, acc_own, max_own, row_d, [(keys[at, :], values[at, :])])

    def early(slots):
        pairs = [(kbuf.at[slot], vbuf.at[slot]) for slot in slots]
        blocks = first_units(pairs)
        unit(q_ref, acc_own, max_own, half, blocks)

    def late(slots):
        third_unit([(kbuf.at[slot], vbuf.at[slot]) for slot in slots])
        for slot in slots:
            last_unit(kbuf.at[slot], vbuf.at[slot], slot)

    for load in loads[:3]:
        load.wait()
    unit(q_ref, acc_own, max_own, 0, [(k_ref[:half, :], v_ref[:half, :])], True)
    unit(q_ref, acc_own, max_own, half, [(k_ref[half:, :], v_ref[half:, :])], True)
    unit(q_ref, acc_own, max_own, half, [(k_ref[:half, :], v_ref[:half, :])])

    def turn(step, carry):
        back = ring - step
        key_copy(k_ref, step, right).wait_recv()
        key_copy(kbuf.at[step], step + 1, right).start()
        key_copy(k_ref, back, left).wait_recv()

        @pl.when(step < top - 1)
        def _():
            key_copy(kbuf.at[back], back - 1, left).start()

        @pl.when(step > 1)
        def _():
            late((step - 1, back + 1))

        @pl.when(step == 1)
        def _():
            q_copy.wait_recv()
            lax.fori_loop(1, n_tp, out_start, 0)
            first_units([(k_ref, v_ref)])
            third_unit([(k_ref, v_ref)])

        value_copy(v_ref, step, right).wait_recv()

        @pl.when(step < top - 1)
        def _():
            value_copy(vbuf.at[step], step + 1, right).start()

        value_copy(v_ref, back, left).wait_recv()
        value_copy(vbuf.at[back], back - 1, left).start()
        early((step, back))
        return carry

    lax.fori_loop(1, top, turn, 0)
    late((top - 1, top + 1))
    key_copy(k_ref, top, right).wait_recv()
    value_copy(v_ref, top, left).wait_recv()
    far = [(kbuf.at[top], vbuf.at[top])]
    blocks = first_units(far)
    third_unit(far)

    def settle(acc, top_ref):
        total = acc[:, LANES:]
        seen = total > 0.0
        inverse = 1.0 / jnp.where(seen, total, 1.0)
        level = jnp.where(seen, top_ref[...] * scale + jnp.log2(jnp.where(seen, total, 1.0)), LOW)
        return acc[:, :LANES] * inverse, level

    diagonal = lax.broadcasted_iota(jnp.int32, (LANES, LANES), 0) == lax.broadcasted_iota(
        jnp.int32, (LANES, LANES), 1
    )
    mean_par, level_par = settle(acc_par, max_par)
    o_send[...] = mean_par.astype(BF16)
    st_send[...] = jnp.zeros_like(st_send)
    for g in range(rows // LANES):
        block = level_par[g * LANES : (g + 1) * LANES, :]
        st_send[g : g + 1, :] = jnp.sum(jnp.where(diagonal, block, 0.0), axis=0, keepdims=True)
    sides = (pl.ds(0, half), pl.ds(half, half))
    st_copy = remote(st_send, st_recv, x_send.at[1], x_recv.at[1], across)
    st_copy.start()
    o_copies = [
        remote(o_send.at[at, :], o_recv.at[at, :], x_send.at[2 + n], x_recv.at[2 + n], across)
        for n, at in enumerate(sides)
    ]
    for copy in o_copies:
        copy.start()
    unit(q_ref, acc_own, max_own, half, blocks)
    last_unit(kbuf.at[top], vbuf.at[top], top)
    mean_own, level_own = settle(acc_own, max_own)
    for load in loads[3:]:
        load.wait()

    def out_arrive(step, carry):
        out_copy(step).wait_recv()
        return carry

    lax.fori_loop(1, n_tp, out_arrive, 0)
    hid_acc[...] = res_ref[...].astype(F32)
    str_acc[...] = jnp.zeros_like(str_acc)
    sq_acc[...] = jnp.zeros_like(sq_acc)
    st_copy.wait_recv()

    def join(side):
        o_copies[side].wait_recv()
        for g in range(side * half // LANES, (side + 1) * half // LANES):
            at = slice(g * LANES, (g + 1) * LANES)
            line = jnp.broadcast_to(st_recv[g : g + 1, :], (LANES, LANES))
            level_other = jnp.sum(jnp.where(diagonal, line, 0.0), axis=1, keepdims=True)
            here = level_own[at, :]
            most = jnp.maximum(here, level_other)
            w_own = jnp.exp2(here - most)
            w_other = jnp.exp2(level_other - most)
            joined = (w_own * mean_own[at, :] + w_other * o_recv[at, :].astype(F32)) / (
                w_own + w_other
            )
            att_all[tp, at, :] = joined.astype(BF16)

    targets = {
        "y": {"tp": tp_at(0, 1, 0)},
        "xp": {"tp": tp_at(1, 0, 0)},
        "xm": {"tp": tp_at(-1, 0, 0)},
        "c": {"tp": tp_at(0, 0, 1)},
    }
    moves = []

    def gather(which, side, buf, consume):
        whole = sides[side]
        head = pl.ds(side * half, quarter)
        tail = pl.ds(side * half + quarter, quarter)
        known = {}

        def copy_of(dx, dy, dc, part, number, to):
            ref = buf.at[tp_at(dx, dy, dc), part, :]
            return remote(
                ref, ref, g_send.at[which, side, number], g_recv.at[which, side, number], targets[to]
            )

        def go(dx, dy, to, part=whole):
            number = len(known)
            known[dx, dy, to] = (number, part)
            copy = copy_of(dx, dy, 0, part, number, to)
            copy.start()
            moves.append(copy)

        def come(dx, dy, to):
            number, part = known[dx, dy, to]
            sx = dx + {"xp": -1, "xm": 1}.get(to, 0)
            sy = 1 - dy if to == "y" else dy
            copy_of(sx, sy, 1 if to == "c" else 0, part, number, to).wait_recv()

        def pair(dx, dy):
            come(dx, dy, "c")
            consume(tp_at(dx, dy, 0) // 2, whole)

        def relay(dx, dy):
            go(dx, dy, "xp" if dx < 0 else "xm", head if dx < 0 else tail)

        def y_first():
            for to in ("y", "xp", "xm", "c"):
                go(0, 0, to)
            yield
            come(0, 0, "y")
            for to in ("xp", "xm", "c"):
                go(0, 1, to)
            pair(0, 0)
            yield
            for dx, to in ((-1, "xp"), (1, "xm")):
                come(0, 0, to)
                relay(dx, 0)
                go(dx, 0, "c")
            yield
            pair(0, 1)
            for dx, to in ((-1, "xp"), (1, "xm")):
                come(0, 1, to)
                relay(dx, 1)
                go(dx, 1, "c")
            yield
            pair(-1, 0)
            pair(1, 0)
            yield
            come(-1, 0, "xp")
            come(1, 0, "xm")
            go(2, 0, "c")
            pair(-1, 1)
            pair(1, 1)
            yield
            come(-1, 1, "xp")
            come(1, 1, "xm")
            go(2, 1, "c")
            pair(2, 0)
            yield
            pair(2, 1)
            yield

        def x_first():
            for to in ("xp", "xm", "y", "c"):
                go(0, 0, to)
            yield
            pair(0, 0)
            for dx, to in ((-1, "xp"), (1, "xm")):
                come(0, 0, to)
                relay(dx, 0)
                go(dx, 0, "y")
                go(dx, 0, "c")
            yield
            come(0, 0, "y")
            go(0, 1, "c")
            pair(-1, 0)
            pair(1, 0)
            yield
            come(-1, 0, "xp")
            come(1, 0, "xm")
            go(2, 0, "y")
            go(2, 0, "c")
            come(-1, 0, "y")
            go(-1, 1, "c")
            come(1, 0, "y")
            go(1, 1, "c")
            yield
            pair(0, 1)
            pair(2, 0)
            yield
            come(2, 0, "y")
            go(2, 1, "c")
            pair(-1, 1)
            pair(1, 1)
            yield
            pair(2, 1)
            yield

        return x_first() if side else y_first()

    def project_out(chip, at):
        left_side = jnp.concatenate([att_all[2 * chip, at, :], att_all[2 * chip + 1, at, :]], axis=1)
        weight = jnp.concatenate([wout[2 * chip], wout[2 * chip + 1]], axis=0)
        hid_acc[at, :] += jnp.dot(left_side, weight, preferred_element_type=F32)

    def project_in(chip, at):
        parts = []
        for c in range(2):
            wide = hid_all[2 * chip + c, at, :].astype(F32)
            sq_acc[at, :] += wide * wide
            parts.append((wide * gain_ref[pl.ds(2 * chip + c, 1), :]).astype(BF16))
        deep = pl.ds(pl.multiple_of(chip * 2 * LANES, 2 * LANES), 2 * LANES)
        str_acc[at, :] += jnp.dot(
            jnp.concatenate(parts, axis=1), win[deep, :], preferred_element_type=F32
        )

    def finish_hidden(side):
        at = sides[side]
        hidden = hid_acc[at, :].astype(BF16)
        hid_all[tp, at, :] = hidden
        hid_ref[at, :] = hidden

    edge = 2 * RIM
    rim_copies = [
        remote(
            str_ref.at[(side + 1) * half - edge : (side + 1) * half, :],
            halo.at[side],
            x_send.at[4 + side],
            x_recv.at[4 + side],
            to,
        )
        for side, to in enumerate((after, before))
    ]

    def finish_streams(side):
        at = sides[side]
        mean_square = jnp.sum(sq_acc[at, :], axis=1, keepdims=True) / (n_tp * LANES)
        streams = (str_acc[at, :] * lax.rsqrt(mean_square + 1e-6)).astype(BF16)
        str_ref[at, :] = streams
        rim_copies[side].start()
        ext[side, RIM:, :] = streams.astype(F32)

    out_a, out_b = gather(0, 0, att_all, project_out), gather(0, 1, att_all, project_out)
    in_a, in_b = gather(1, 0, hid_all, project_in), gather(1, 1, hid_all, project_in)
    join(0)
    next(out_a)
    join(1)
    next(out_b)
    order = ["a", "a", "b", "b", "a", "a", "a", "b", "a", "b", "a"]
    for name in order:
        next(out_a if name == "a" else out_b)
    finish_hidden(0)
    next(in_a)
    next(out_b)
    next(out_b)
    finish_hidden(1)
    next(in_b)
    for name in order:
        next(in_a if name == "a" else in_b)
    finish_streams(0)
    next(in_b)
    next(in_b)
    finish_streams(1)

    lane_group = lax.broadcasted_iota(jnp.int32, (FILTER_TAPS, LANES), 1) // GROUP
    filt = jnp.zeros((FILTER_TAPS, LANES), F32)
    for g in range(LANES // GROUP):
        filt = jnp.where(lane_group == g, filt_ref[:, g : g + 1], filt)

    def convolve(side, low, high):
        count = high - low
        span = count + FILTER_TAPS - 1

        def featured(stream, first, number):
            cols = slice(stream * LANES, (stream + 1) * LANES)
            total = None
            for j in range(FEAT_TAPS):
                row = first + RIM - j
                term = taps_ref[j, stream : stream + 1, :] * ext[side, row : row + number, cols]
                total = term if total is None else total + term
            return total

        first = low - (FILTER_TAPS - 1)
        mix[0:span, :] = featured(0, first, span) * featured(2, first, span)
        response = None
        for j in range(FILTER_TAPS):
            row = FILTER_TAPS - 1 - j
            term = filt[j : j + 1, :] * mix[row : row + count, :]
            response = term if response is None else response + term
        out = featured(1, low, count) * response
        gated_ref[side * half + low : side * half + high, :] = out.astype(BF16)

    convolve(0, edge, half)
    convolve(1, edge, half)
    rim_copies[0].wait_recv()
    ext[0, :RIM, :] = jnp.where(dev == 0, 0.0, halo[0].astype(F32)[RIM:])
    convolve(0, 0, edge)
    rim_copies[1].wait_recv()
    first_tail = str_ref[half - edge : half, :].astype(F32)[RIM:]
    ext[1, :RIM, :] = jnp.where(dev == n_ctx - 1, first_tail, halo[1].astype(F32)[RIM:])
    convolve(1, 0, edge)

    def drain(slot, carry):
        key_copy(k_ref, slot, right).wait_send()
        value_copy(v_ref, slot, right).wait_send()
        return carry

    lax.fori_loop(1, ring, drain, 0)

    def out_drain(step, carry):
        out_copy(step).wait_send()
        return carry

    lax.fori_loop(1, n_tp, out_drain, 0)
    for copy in [q_copy, st_copy] + o_copies + rim_copies + moves:
        copy.wait_send()


def local(queries, keys, values, residual, out_proj, norm_gain, in_proj, feat_taps, long_filter):
    rows, width = queries.shape
    half = rows // 2
    n_tp = lax.axis_size("tp")
    ring = lax.axis_size("ctx") // 2
    vmem = pl.BlockSpec(memory_space=pltpu.VMEM)
    hbm = pl.BlockSpec(memory_space=pltpu.HBM)
    dma = pltpu.SemaphoreType.DMA
    shape = jax.ShapeDtypeStruct((rows, width), BF16)
    return pl.pallas_call(
        functools.partial(kernel, ring),
        out_shape=(shape, shape),
        in_specs=[hbm] * 9,
        out_specs=(vmem, vmem),
        scratch_shapes=[
            pltpu.VMEM((rows, width), BF16),
            pltpu.VMEM((rows, width), BF16),
            pltpu.VMEM((rows, width), BF16),
            pltpu.VMEM((rows, width), BF16),
            pltpu.VMEM((n_tp, LANES), F32),
            pltpu.VMEM((FEAT_TAPS, 3, LANES), F32),
            pltpu.VMEM((FILTER_TAPS, LANES // GROUP), F32),
            pltpu.VMEM((ring, rows, width), BF16),
            pltpu.VMEM((ring, rows, width), BF16),
            pltpu.VMEM((rows, width), BF16),
            pltpu.VMEM((rows, 2 * width), F32),
            pltpu.VMEM((rows, 2 * width), F32),
            pltpu.VMEM((rows, width), F32),
            pltpu.VMEM((rows, width), F32),
            pltpu.VMEM((rows, width), BF16),
            pltpu.VMEM((rows, width), BF16),
            pltpu.VMEM((8, LANES), F32),
            pltpu.VMEM((8, LANES), F32),
            pltpu.VMEM((n_tp, LANES, LANES), BF16),
            pltpu.VMEM((n_tp * LANES, 3 * LANES), BF16),
            pltpu.VMEM((n_tp, rows, width), BF16),
            pltpu.VMEM((n_tp, rows, width), BF16),
            pltpu.VMEM((rows, LANES), F32),
            pltpu.VMEM((rows, 3 * LANES), F32),
            pltpu.VMEM((rows, LANES), F32),
            pltpu.VMEM((rows, 3 * LANES), BF16),
            pltpu.VMEM((2, 2 * RIM, 3 * LANES), BF16),
            pltpu.VMEM((2, RIM + half, 3 * LANES), F32),
            pltpu.VMEM((RIM + half, LANES), F32),
            dma((11,)),
            dma((ring,)),
            dma((ring,)),
            dma((ring,)),
            dma((ring,)),
            dma((6,)),
            dma((6,)),
            dma((n_tp,)),
            dma((n_tp,)),
            dma((2, 2, 17)),
            dma((2, 2, 17)),
        ],
        compiler_params=pltpu.CompilerParams(
            collective_id=0, has_side_effects=True, vmem_limit_bytes=60 * 1024 * 1024
        ),
        cost_estimate=pl.CostEstimate(
            flops=4 * 10**9, bytes_accessed=4 * 10**6, transcendentals=5 * 10**6
        ),
    )(
        queries,
        keys,
        values,
        residual,
        out_proj,
        norm_gain.reshape(n_tp, LANES),
        jnp.transpose(in_proj, (1, 0, 2)),
        feat_taps,
        long_filter,
    )


def solution(mesh):
    return jax.shard_map(
        local,
        mesh=mesh,
        in_specs=(
            P("ctx", "tp"),
            P("ctx", "tp"),
            P("ctx", "tp"),
            P("ctx", "tp"),
            P("tp", None),
            P(),
            P(None, None, "tp"),
            P(None, None, "tp"),
            P(None, "tp"),
        ),
        out_specs=(P("ctx", "tp"), P("ctx", "tp")),
        check_vma=False,
    )
```

time: 118 us -> 101 us (0.86)
  Pallas kernels: 107 us -> 96.8 us
  local copies, waits for them, and re-layouts: 9.44 us -> 3.14 us
    pallas_call x1, Pallas kernels: 107 us -> 96.8 us  [local(): pl.pallas_call(functools.partial(kernel, ring), out_shape=(shape, shape),...]
    unnamed x20 -> x2, local copies, waits for them, and re-layouts: 9.44 us -> 3.14 us
where the time goes in v2:
time: 101 us
  Pallas kernels  96.8 us (96%)
  local copies, waits for them, and re-layouts  3.14 us (3%)
    pallas_call x1, Pallas kernels, local(): pl.pallas_call(functools.partial(kernel, ring), out_shape=(shape, shape),...  96.8 us
    unnamed x2, local copies, waits for them, and re-layouts  3.14 us

profile of v2, /device:TPU:1, one launch (start us, length us, event | category | flops | bytes accessed | tf_op | source)
XLA Modules:
  0.0 100.6 jit_solution(2357451655605371900)
XLA Ops:
  0.6 96.8 %shard_map.104 = (bf16[512,128]{1,0:T(8,128)(2,1)}, bf16[512,128]{1,0:T(8,128)(2,1)}) custom-call(bf16[512,128]{1,0:T(8,128)(2,1)} %q_hbm.1, bf16[512,128]{1,0:T(8,128)(2,1)} %k_hbm.1, bf16[512,128]{1,0:T(8,128)(2,1)} %v_hbm.1, bf16[512,128]{1,0:T(8,128)(2,1)} %res_hbm.1, bf16[128,2048]{1,0:T(8,128)(2,1)} %outp_hbm.1, f32[16,128]{1,0:T(8,128)} %bitcast.3, ...), custom_call_target="tpu_custom_call" | custom-call | flops 4000000000 | bytes 4000000 | tf_op jit(solution)/shard_map/pallas_call | solution.py:567
  97.5 1.6 %copy.13 = bf16[512,128]{1,0:T(8,128)(2,1)} copy(bf16[512,128]{1,0:T(8,128)(2,1)} %get-tuple-element.4) | data formatting | bytes 262144
  99.0 1.6 %copy.14 = bf16[512,128]{1,0:T(8,128)(2,1)} copy(bf16[512,128]{1,0:T(8,128)(2,1)} %get-tuple-element.5) | data formatting | bytes 262144

commit v3 on v2

--- a/solution.py
+++ b/solution.py
@@ -35,7 +35,6 @@
     q_ref,
     k_ref,
     v_ref,
-    res_ref,
     gain_ref,
     taps_ref,
     filt_ref,
@@ -50,13 +49,14 @@
     o_recv,
     st_send,
     st_recv,
-    wout,
+    wo_all,
     win,
+    joint,
     att_all,
-    hid_all,
+    res_all,
     hid_acc,
     str_acc,
-    sq_acc,
+    sq_all,
     str_ref,
     halo,
     ext,
@@ -78,7 +78,7 @@
     quarter = half // 2
     top = ring // 2
     n_ctx = 2 * ring
-    n_tp = wout.shape[0]
+    n_tp = att_all.shape[0]
     n_x = n_tp // 4
     dev = lax.axis_index("ctx")
     y_hi = dev // ring
@@ -117,16 +117,20 @@
     lax.fori_loop(1, n_tp, greet, 0)
 
     own_cols = pl.ds(pl.multiple_of(tp * LANES, LANES), LANES)
+
+    def head_rows(head, first=0, count=LANES):
+        return pl.ds(pl.multiple_of(head * LANES + first, count), count)
+
     loads = []
     for src, dst in [
         (q_hbm, q_ref),
         (k_hbm, k_ref),
         (v_hbm, v_ref),
-        (res_hbm, res_ref),
+        (res_hbm, res_all.at[tp]),
+        (outp_hbm, wo_all.at[head_rows(tp), :]),
         (gain_hbm, gain_ref),
         (taps_hbm, taps_ref),
         (filt_hbm, filt_ref),
-        (outp_hbm.at[:, own_cols], wout.at[tp]),
     ] + [(inp_hbm.at[s], win.at[:, s * LANES : (s + 1) * LANES]) for s in range(3)]:
         load = pltpu.make_async_copy(src, dst, in_sem.at[len(loads)])
         load.start()
@@ -155,16 +159,119 @@
     value_copy(v_hbm, 1, right).start()
     value_copy(v_hbm, ring - 1, left).start()
 
-    def out_copy(step):
-        peer = lax.rem(tp + step, n_tp)
-        cols = pl.ds(pl.multiple_of(peer * LANES, LANES), LANES)
-        return remote(
-            outp_hbm.at[:, cols], wout.at[tp], w_send.at[step], w_recv.at[step], {"tp": peer}
-        )
-
-    def out_start(step, carry):
-        out_copy(step).start()
-        return carry
+    targets = {
+        "y": {"tp": tp_at(0, 1, 0)},
+        "xp": {"tp": tp_at(1, 0, 0)},
+        "xm": {"tp": tp_at(-1, 0, 0)},
+        "c": {"tp": tp_at(0, 0, 1)},
+    }
+    moves = []
+
+    def gather(which, side, place, span, consume):
+        whole = (side * span, span)
+        head = (side * span, span // 2)
+        tail = (side * span + span // 2, span // 2)
+        known = {}
+
+        def copy_of(dx, dy, dc, part, number, to):
+            ref = place(tp_at(dx, dy, dc), *part)
+            return remote(
+                ref, ref, g_send.at[which, side, number], g_recv.at[which, side, number], targets[to]
+            )
+
+        def go(dx, dy, to, part=whole):
+            number = len(known)
+            known[dx, dy, to] = (number, part)
+            copy_of(dx, dy, 0, part, number, to).start()
+            moves.append(lambda: copy_of(dx, dy, 0, part, number, to))
+
+        def come(dx, dy, to):
+            number, part = known[dx, dy, to]
+            sx = dx + {"xp": -1, "xm": 1}.get(to, 0)
+            sy = 1 - dy if to == "y" else dy
+            copy_of(sx, sy, 1 if to == "c" else 0, part, number, to).wait_recv()
+
+        def pair(dx, dy):
+            come(dx, dy, "c")
+            consume(tp_at(dx, dy, 0) // 2)
+
+        def relay(dx, dy):
+            go(dx, dy, "xp" if dx < 0 else "xm", head if dx < 0 else tail)
+
+        def y_first():
+            for to in ("y", "xp", "xm", "c"):
+                go(0, 0, to)
+            yield
+            come(0, 0, "y")
+            for to in ("xp", "xm", "c"):
+                go(0, 1, to)
+            pair(0, 0)
+            yield
+            for dx, to in ((-1, "xp"), (1, "xm")):
+                come(0, 0, to)
+                relay(dx, 0)
+                go(dx, 0, "c")
+            yield
+            pair(0, 1)
+            for dx, to in ((-1, "xp"), (1, "xm")):
+                come(0, 1, to)
+                relay(dx, 1)
+                go(dx, 1, "c")
+            yield
+            pair(-1, 0)
+            pair(1, 0)
+            yield
+            come(-1, 0, "xp")
+            come(1, 0, "xm")
+            go(2, 0, "c")
+            pair(-1, 1)
+            pair(1, 1)
+            yield
+            come(-1, 1, "xp")
+            come(1, 1, "xm")
+            go(2, 1, "c")
+            pair(2, 0)
+            yield
+            pair(2, 1)
+            yield
+
+        def x_first():
+            for to in ("xp", "xm", "y", "c"):
+                go(0, 0, to)
+            yield
+            pair(0, 0)
+            for dx, to in ((-1, "xp"), (1, "xm")):
+                come(0, 0, to)
+                relay(dx, 0)
+                go(dx, 0, "y")
+                go(dx, 0, "c")
+            yield
+            come(0, 0, "y")
+            go(0, 1, "c")
+            pair(-1, 0)
+            pair(1, 0)
+            yield
+            come(-1, 0, "xp")
+            come(1, 0, "xm")
+            go(2, 0, "y")
+            go(2, 0, "c")
+            come(-1, 0, "y")
+            go(-1, 1, "c")
+            come(1, 0, "y")
+            go(1, 1, "c")
+            yield
+            pair(0, 1)
+            pair(2, 0)
+            yield
+            come(2, 0, "y")
+            go(2, 1, "c")
+            pair(-1, 1)
+            pair(1, 1)
+            yield
+            pair(2, 1)
+            yield
+
+        return x_first() if side else y_first()
 
     ones = jnp.ones((half, LANES), BF16)
     tri = lax.broadcasted_iota(jnp.int32, (half, half), 0) >= lax.broadcasted_iota(
@@ -220,8 +327,82 @@
         for slot in slots:
             last_unit(kbuf.at[slot], vbuf.at[slot], slot)
 
-    for load in loads[:3]:
+    for load in loads[:5]:
         load.wait()
+
+    def res_place(chunk, first, count):
+        return res_all.at[chunk, pl.ds(first, count), :]
+
+    def wo_place(chunk, first, count):
+        return wo_all.at[head_rows(chunk, first, count), :]
+
+    def att_place(chunk, first, count):
+        return att_all.at[chunk, pl.ds(first, count), :]
+
+    def nothing(chip):
+        pass
+
+    res_a = gather(1, 0, res_place, half, nothing)
+    res_b = gather(1, 1, res_place, half, nothing)
+    wo_a = gather(2, 0, wo_place, LANES // 2, nothing)
+    wo_b = gather(2, 1, wo_place, LANES // 2, nothing)
+    for stages in (res_a, res_b, wo_a, wo_b):
+        next(stages)
+    for load in loads[5:]:
+        load.wait()
+    str_acc[...] = jnp.zeros_like(str_acc)
+    diagonal = lax.broadcasted_iota(jnp.int32, (LANES, LANES), 0) == lax.broadcasted_iota(
+        jnp.int32, (LANES, LANES), 1
+    )
+
+    def to_column(line):
+        return jnp.sum(jnp.where(diagonal, line, 0.0), axis=1, keepdims=True)
+
+    def to_line(column):
+        return jnp.sum(jnp.where(diagonal, column, 0.0), axis=0, keepdims=True)
+
+    def scale_win():
+        def block(head, carry):
+            at = head_rows(head)
+            column = to_column(gain_ref[pl.ds(head, 1), :])
+            win[at, :] = (win[at, :].astype(F32) * column).astype(BF16)
+            return carry
+
+        lax.fori_loop(0, n_tp, block, 0)
+
+    def chip_rows(chip):
+        return pl.ds(pl.multiple_of(chip * 2 * LANES, 2 * LANES), 2 * LANES)
+
+    def prepare(*offsets):
+        for dx, dy in offsets:
+            chip = tp_at(dx, dy, 0) // 2
+            deep = chip_rows(chip)
+            joint[deep, :] = jnp.dot(
+                wo_all[deep, :], win[...], preferred_element_type=F32
+            ).astype(BF16)
+            left_side = jnp.concatenate([res_all[2 * chip], res_all[2 * chip + 1]], axis=1)
+            str_acc[...] += jnp.dot(left_side, win[deep, :], preferred_element_type=F32)
+
+    def steps(*names):
+        for stages in names:
+            next(stages)
+
+    plan = {
+        1: ((res_a, res_a, res_b), ()),
+        2: ((wo_a, wo_a, wo_b, res_a, res_a, res_b), ()),
+        3: ((res_a, res_b), ()),
+        4: ((wo_b, wo_a, wo_a, res_a, res_b), ()),
+        5: ((wo_a, wo_b, res_a, res_b), ()),
+        6: ((wo_a, wo_b, res_b), ((0, 0), (0, 1))),
+        7: ((wo_a, wo_b), ((-1, 0), (1, 0))),
+    }
+
+    def extra(number):
+        names, offsets = plan[number]
+        steps(*names)
+        prepare(*offsets)
+        if number == 3:
+            scale_win()
     unit(q_ref, acc_own, max_own, 0, [(k_ref[:half, :], v_ref[:half, :])], True)
     unit(q_ref, acc_own, max_own, half, [(k_ref[half:, :], v_ref[half:, :])], True)
     unit(q_ref, acc_own, max_own, half, [(k_ref[:half, :], v_ref[:half, :])])
@@ -243,7 +424,6 @@
         @pl.when(step == 1)
         def _():
             q_copy.wait_recv()
-            lax.fori_loop(1, n_tp, out_start, 0)
             first_units([(k_ref, v_ref)])
             third_unit([(k_ref, v_ref)])
 
@@ -256,9 +436,13 @@
         value_copy(v_ref, back, left).wait_recv()
         value_copy(vbuf.at[back], back - 1, left).start()
         early((step, back))
+        for number in range(1, top):
+            pl.when(step == number)(functools.partial(extra, number))
         return carry
 
     lax.fori_loop(1, top, turn, 0)
+    for number in range(top, 8):
+        extra(number)
     late((top - 1, top + 1))
     key_copy(k_ref, top, right).wait_recv()
     value_copy(v_ref, top, left).wait_recv()
@@ -273,15 +457,12 @@
         level = jnp.where(seen, top_ref[...] * scale + jnp.log2(jnp.where(seen, total, 1.0)), LOW)
         return acc[:, :LANES] * inverse, level
 
-    diagonal = lax.broadcasted_iota(jnp.int32, (LANES, LANES), 0) == lax.broadcasted_iota(
-        jnp.int32, (LANES, LANES), 1
-    )
     mean_par, level_par = settle(acc_par, max_par)
     o_send[...] = mean_par.astype(BF16)
     st_send[...] = jnp.zeros_like(st_send)
     for g in range(rows // LANES):
         block = level_par[g * LANES : (g + 1) * LANES, :]
-        st_send[g : g + 1, :] = jnp.sum(jnp.where(diagonal, block, 0.0), axis=0, keepdims=True)
+        st_send[g : g + 1, :] = to_line(block)
     sides = (pl.ds(0, half), pl.ds(half, half))
     st_copy = remote(st_send, st_recv, x_send.at[1], x_recv.at[1], across)
     st_copy.start()
@@ -294,25 +475,16 @@
     unit(q_ref, acc_own, max_own, half, blocks)
     last_unit(kbuf.at[top], vbuf.at[top], top)
     mean_own, level_own = settle(acc_own, max_own)
-    for load in loads[3:]:
-        load.wait()
-
-    def out_arrive(step, carry):
-        out_copy(step).wait_recv()
-        return carry
-
-    lax.fori_loop(1, n_tp, out_arrive, 0)
-    hid_acc[...] = res_ref[...].astype(F32)
-    str_acc[...] = jnp.zeros_like(str_acc)
-    sq_acc[...] = jnp.zeros_like(sq_acc)
+    steps(wo_b)
+    prepare((-1, 1), (1, 1), (2, 0), (2, 1))
+    hid_acc[...] = res_all[tp].astype(F32)
     st_copy.wait_recv()
 
     def join(side):
         o_copies[side].wait_recv()
         for g in range(side * half // LANES, (side + 1) * half // LANES):
             at = slice(g * LANES, (g + 1) * LANES)
-            line = jnp.broadcast_to(st_recv[g : g + 1, :], (LANES, LANES))
-            level_other = jnp.sum(jnp.where(diagonal, line, 0.0), axis=1, keepdims=True)
+            level_other = to_column(st_recv[g : g + 1, :])
             here = level_own[at, :]
             most = jnp.maximum(here, level_other)
             w_own = jnp.exp2(here - most)
@@ -322,142 +494,43 @@
             )
             att_all[tp, at, :] = joined.astype(BF16)
 
-    targets = {
-        "y": {"tp": tp_at(0, 1, 0)},
-        "xp": {"tp": tp_at(1, 0, 0)},
-        "xm": {"tp": tp_at(-1, 0, 0)},
-        "c": {"tp": tp_at(0, 0, 1)},
-    }
-    moves = []
-
-    def gather(which, side, buf, consume):
-        whole = sides[side]
-        head = pl.ds(side * half, quarter)
-        tail = pl.ds(side * half + quarter, quarter)
-        known = {}
-
-        def copy_of(dx, dy, dc, part, number, to):
-            ref = buf.at[tp_at(dx, dy, dc), part, :]
-            return remote(
-                ref, ref, g_send.at[which, side, number], g_recv.at[which, side, number], targets[to]
+    def project(side):
+        at = sides[side]
+
+        def apply(chip):
+            left_side = jnp.concatenate(
+                [att_all[2 * chip, at, :], att_all[2 * chip + 1, at, :]], axis=1
             )
-
-        def go(dx, dy, to, part=whole):
-            number = len(known)
-            known[dx, dy, to] = (number, part)
-            copy = copy_of(dx, dy, 0, part, number, to)
-            copy.start()
-            moves.append(copy)
-
-        def come(dx, dy, to):
-            number, part = known[dx, dy, to]
-            sx = dx + {"xp": -1, "xm": 1}.get(to, 0)
-            sy = 1 - dy if to == "y" else dy
-            copy_of(sx, sy, 1 if to == "c" else 0, part, number, to).wait_recv()
-
-        def pair(dx, dy):
-            come(dx, dy, "c")
-            consume(tp_at(dx, dy, 0) // 2, whole)
-
-        def relay(dx, dy):
-            go(dx, dy, "xp" if dx < 0 else "xm", head if dx < 0 else tail)
-
-        def y_first():
-            for to in ("y", "xp", "xm", "c"):
-                go(0, 0, to)
-            yield
-            come(0, 0, "y")
-            for to in ("xp", "xm", "c"):
-                go(0, 1, to)
-            pair(0, 0)
-            yield
-            for dx, to in ((-1, "xp"), (1, "xm")):
-                come(0, 0, to)
-                relay(dx, 0)
-                go(dx, 0, "c")
-            yield
-            pair(0, 1)
-            for dx, to in ((-1, "xp"), (1, "xm")):
-                come(0, 1, to)
-                relay(dx, 1)
-                go(dx, 1, "c")
-            yield
-            pair(-1, 0)
-            pair(1, 0)
-            yield
-            come(-1, 0, "xp")
-            come(1, 0, "xm")
-            go(2, 0, "c")
-            pair(-1, 1)
-            pair(1, 1)
-            yield
-            come(-1, 1, "xp")
-            come(1, 1, "xm")
-            go(2, 1, "c")
-            pair(2, 0)
-            yield
-            pair(2, 1)
-            yield
-
-        def x_first():
-            for to in ("xp", "xm", "y", "c"):
-                go(0, 0, to)
-            yield
-            pair(0, 0)
-            for dx, to in ((-1, "xp"), (1, "xm")):
-                come(0, 0, to)
-                relay(dx, 0)
-                go(dx, 0, "y")
-                go(dx, 0, "c")
-            yield
-            come(0, 0, "y")
-            go(0, 1, "c")
-            pair(-1, 0)
-            pair(1, 0)
-            yield
-            come(-1, 0, "xp")
-            come(1, 0, "xm")
-            go(2, 0, "y")
-            go(2, 0, "c")
-            come(-1, 0, "y")
-            go(-1, 1, "c")
-            come(1, 0, "y")
-            go(1, 1, "c")
-            yield
-            pair(0, 1)
-            pair(2, 0)
-            yield
-            come(2, 0, "y")
-            go(2, 1, "c")
-            pair(-1, 1)
-            pair(1, 1)
-            yield
-            pair(2, 1)
-            yield
-
-        return x_first() if side else y_first()
-
-    def project_out(chip, at):
-        left_side = jnp.concatenate([att_all[2 * chip, at, :], att_all[2 * chip + 1, at, :]], axis=1)
-        weight = jnp.concatenate([wout[2 * chip], wout[2 * chip + 1]], axis=0)
-        hid_acc[at, :] += jnp.dot(left_side, weight, preferred_element_type=F32)
-
-    def project_in(chip, at):
-        parts = []
-        for c in range(2):
-            wide = hid_all[2 * chip + c, at, :].astype(F32)
-            sq_acc[at, :] += wide * wide
-            parts.append((wide * gain_ref[pl.ds(2 * chip + c, 1), :]).astype(BF16))
-        deep = pl.ds(pl.multiple_of(chip * 2 * LANES, 2 * LANES), 2 * LANES)
-        str_acc[at, :] += jnp.dot(
-            jnp.concatenate(parts, axis=1), win[deep, :], preferred_element_type=F32
-        )
+            deep = chip_rows(chip)
+            weight = jnp.concatenate([wo_all[deep, own_cols], joint[deep, :]], axis=1)
+            product = jnp.dot(left_side, weight, preferred_element_type=F32)
+            hid_acc[at, :] += product[:, :LANES]
+            str_acc[at, :] += product[:, LANES:]
+
+        return apply
+
+    def square_copy(side, step):
+        peer = lax.rem(tp + step, n_tp)
+        ref = sq_all.at[tp, side]
+        return remote(ref, ref, w_send.at[side, step], w_recv.at[side, step], {"tp": peer})
+
+    def square_each(side, act):
+        def one(step, carry):
+            act(square_copy(side, step))
+            return carry
+
+        lax.fori_loop(1, n_tp, one, 0)
 
     def finish_hidden(side):
         at = sides[side]
         hidden = hid_acc[at, :].astype(BF16)
-        hid_all[tp, at, :] = hidden
         hid_ref[at, :] = hidden
+        wide = hidden.astype(F32)
+        column = jnp.sum(wide * wide, axis=1, keepdims=True)
+        sq_all[tp, side] = jnp.zeros((8, LANES), F32)
+        for g in range(half // LANES):
+            sq_all[tp, side, g : g + 1, :] = to_line(column[g * LANES : (g + 1) * LANES])
+        square_each(side, lambda copy: copy.start())
 
     edge = 2 * RIM
     rim_copies = [
@@ -472,33 +545,27 @@
     ]
 
     def finish_streams(side):
-        at = sides[side]
-        mean_square = jnp.sum(sq_acc[at, :], axis=1, keepdims=True) / (n_tp * LANES)
-        streams = (str_acc[at, :] * lax.rsqrt(mean_square + 1e-6)).astype(BF16)
-        str_ref[at, :] = streams
+        square_each(side, lambda copy: copy.wait_recv())
+        lines = jnp.sum(sq_all[:, side], axis=0)
+        for g in range(half // LANES):
+            at = slice(side * half + g * LANES, side * half + (g + 1) * LANES)
+            mean_square = to_column(lines[g : g + 1, :]) / (n_tp * LANES)
+            streams = (str_acc[at, :] * lax.rsqrt(mean_square + 1e-6)).astype(BF16)
+            str_ref[at, :] = streams
+            ext[side, RIM + g * LANES : RIM + (g + 1) * LANES, :] = streams.astype(F32)
         rim_copies[side].start()
-        ext[side, RIM:, :] = streams.astype(F32)
-
-    out_a, out_b = gather(0, 0, att_all, project_out), gather(0, 1, att_all, project_out)
-    in_a, in_b = gather(1, 0, hid_all, project_in), gather(1, 1, hid_all, project_in)
+
+    out_a = gather(0, 0, att_place, half, project(0))
+    out_b = gather(0, 1, att_place, half, project(1))
     join(0)
     next(out_a)
     join(1)
     next(out_b)
-    order = ["a", "a", "b", "b", "a", "a", "a", "b", "a", "b", "a"]
-    for name in order:
-        next(out_a if name == "a" else out_b)
+    steps(out_a, out_a, out_b, out_b, out_a, out_a, out_a, out_b, out_a, out_b, out_a)
     finish_hidden(0)
-    next(in_a)
-    next(out_b)
-    next(out_b)
+    steps(out_b, out_b)
     finish_hidden(1)
-    next(in_b)
-    for name in order:
-        next(in_a if name == "a" else in_b)
     finish_streams(0)
-    next(in_b)
-    next(in_b)
     finish_streams(1)
 
     lane_group = lax.broadcasted_iota(jnp.int32, (FILTER_TAPS, LANES), 1) // GROUP
@@ -546,13 +613,12 @@
 
     lax.fori_loop(1, ring, drain, 0)
 
-    def out_drain(step, carry):
-        out_copy(step).wait_send()
-        return carry
-
-    lax.fori_loop(1, n_tp, out_drain, 0)
-    for copy in [q_copy, st_copy] + o_copies + rim_copies + moves:
+    for side in range(2):
+        square_each(side, lambda copy: copy.wait_send())
+    for copy in [q_copy, st_copy] + o_copies + rim_copies:
         copy.wait_send()
+    for move in moves:
+        move().wait_send()
 
 
 def local(queries, keys, values, residual, out_proj, norm_gain, in_proj, feat_taps, long_filter):
@@ -573,7 +639,6 @@
             pltpu.VMEM((rows, width), BF16),
             pltpu.VMEM((rows, width), BF16),
             pltpu.VMEM((rows, width), BF16),
-            pltpu.VMEM((rows, width), BF16),
             pltpu.VMEM((n_tp, LANES), F32),
             pltpu.VMEM((FEAT_TAPS, 3, LANES), F32),
             pltpu.VMEM((FILTER_TAPS, LANES // GROUP), F32),
@@ -588,13 +653,14 @@
             pltpu.VMEM((rows, width), BF16),
             pltpu.VMEM((8, LANES), F32),
             pltpu.VMEM((8, LANES), F32),
-            pltpu.VMEM((n_tp, LANES, LANES), BF16),
+            pltpu.VMEM((n_tp * LANES, n_tp * LANES), BF16),
+            pltpu.VMEM((n_tp * LANES, 3 * LANES), BF16),
             pltpu.VMEM((n_tp * LANES, 3 * LANES), BF16),
             pltpu.VMEM((n_tp, rows, width), BF16),
             pltpu.VMEM((n_tp, rows, width), BF16),
             pltpu.VMEM((rows, LANES), F32),
             pltpu.VMEM((rows, 3 * LANES), F32),
-            pltpu.VMEM((rows, LANES), F32),
+            pltpu.VMEM((n_tp, 2, 8, LANES), F32),
             pltpu.VMEM((rows, 3 * LANES), BF16),
             pltpu.VMEM((2, 2 * RIM, 3 * LANES), BF16),
             pltpu.VMEM((2, RIM + half, 3 * LANES), F32),
@@ -606,27 +672,32 @@
             dma((ring,)),
             dma((6,)),
             dma((6,)),
-            dma((n_tp,)),
-            dma((n_tp,)),
-            dma((2, 2, 17)),
-            dma((2, 2, 17)),
+            dma((2, n_tp)),
+            dma((2, n_tp)),
+            dma((3, 2, 17)),
+            dma((3, 2, 17)),
         ],
         compiler_params=pltpu.CompilerParams(
-            collective_id=0, has_side_effects=True, vmem_limit_bytes=60 * 1024 * 1024
+            collective_id=0, has_side_effects=True, vmem_limit_bytes=40 * 1024 * 1024
         ),
         cost_estimate=pl.CostEstimate(
             flops=4 * 10**9, bytes_accessed=4 * 10**6, transcendentals=5 * 10**6
         ),
     )(
-        queries,
-        keys,
-        values,
-        residual,
-        out_proj,
-        norm_gain.reshape(n_tp, LANES),
-        jnp.transpose(in_proj, (1, 0, 2)),
-        feat_taps,
-        long_filter,
+        *(
+            pltpu.with_memory_space_constraint(operand, pltpu.HBM)
+            for operand in (
+                queries,
+                keys,
+                values,
+                residual,
+                out_proj,
+                norm_gain.reshape(n_tp, LANES),
+                jnp.transpose(in_proj, (1, 0, 2)),
+                feat_taps,
+                long_filter,
+            )
+        )
     )
 
 

time: 101 us -> 95.3 us (0.944)
  Pallas kernels: 96.8 us -> 93.2 us
  local copies, waits for them, and re-layouts: 3.14 us -> 1.31 us
    pallas_call x1, Pallas kernels: 96.8 us -> 93.2 us  [local(): pl.pallas_call(functools.partial(kernel, ring), out_shape=(shape, shape),...]
    unnamed x2, local copies, waits for them, and re-layouts: 3.14 us -> 1.31 us
where the time goes in v3:
time: 95.3 us; the launch traced here: 95.2 us
  Pallas kernels  93.2 us (98%)
  local copies, waits for them, and re-layouts  1.31 us (1%)
    pallas_call x1, Pallas kernels, local(): pl.pallas_call(functools.partial(kernel, ring), out_shape=(shape, shape),...  93.2 us

profile of v3, /device:TPU:1, one launch (start us, length us, event | category | flops | bytes accessed | tf_op | source)
XLA Modules:
  0.0 95.2 jit_solution(5494868122926910990)
XLA Ops:
  0.6 93.2 %shard_map.104 = (bf16[512,128]{1,0:T(8,128)(2,1)S(1)}, bf16[512,128]{1,0:T(8,128)(2,1)S(1)}) custom-call(bf16[512,128]{1,0:T(8,128)(2,1)} %q_hbm.1, bf16[512,128]{1,0:T(8,128)(2,1)} %k_hbm.1, bf16[512,128]{1,0:T(8,128)(2,1)} %v_hbm.1, bf16[512,128]{1,0:T(8,128)(2,1)} %res_hbm.1, bf16[128,2048]{1,0:T(8,128)(2,1)} %outp_hbm.1, f32[16,128]{1,0:T(8,128)} %bitcast.3, ...), custom_call_target="tpu_custom_call" | custom-call | flops 4000000000 | bytes 4000000 | tf_op jit(solution)/shard_map/pallas_call | solution.py:633
  93.9 0.7 copy.13
  94.5 0.7 copy.14

commit v4 on v3

--- a/solution.py
+++ b/solution.py
@@ -57,8 +57,6 @@
     hid_acc,
     str_acc,
     sq_all,
-    str_ref,
-    halo,
     ext,
     mix,
     in_sem,
@@ -70,12 +68,15 @@
     x_recv,
     w_send,
     w_recv,
+    h_send,
+    h_recv,
     g_send,
     g_recv,
 ):
     rows, width = q_ref.shape
     half = rows // 2
-    quarter = half // 2
+    edge = 2 * RIM
+    rim = pl.ds(rows, 2 * edge)
     top = ring // 2
     n_ctx = 2 * ring
     n_tp = att_all.shape[0]
@@ -126,7 +127,7 @@
         (q_hbm, q_ref),
         (k_hbm, k_ref),
         (v_hbm, v_ref),
-        (res_hbm, res_all.at[tp]),
+        (res_hbm, res_all.at[tp, pl.ds(0, rows), :]),
         (outp_hbm, wo_all.at[head_rows(tp), :]),
         (gain_hbm, gain_ref),
         (taps_hbm, taps_ref),
@@ -146,18 +147,50 @@
             src_ref=src, dst_ref=dst, send_sem=send, recv_sem=recv, device_id=to, device_id_type=MESH
         )
 
-    def key_copy(src, slot, to):
-        return remote(src, kbuf.at[slot], ks_sem.at[slot], kr_sem.at[slot], to)
-
-    def value_copy(src, slot, to):
-        return remote(src, vbuf.at[slot], vs_sem.at[slot], vr_sem.at[slot], to)
-
-    key_copy(k_hbm, 1, right).start()
-    key_copy(k_hbm, ring - 1, left).start()
+    def part_of(ref, side):
+        return ref.at[pl.ds(side * half, half), :]
+
+    def key_copy(src, slot, side, to):
+        dst = part_of(kbuf.at[slot], side)
+        return remote(src, dst, ks_sem.at[slot, side], kr_sem.at[slot, side], to)
+
+    def value_copy(src, slot, side, to):
+        dst = part_of(vbuf.at[slot], side)
+        return remote(src, dst, vs_sem.at[slot, side], vr_sem.at[slot, side], to)
+
     q_copy = remote(q_hbm, qpar, x_send.at[0], x_recv.at[0], across)
-    q_copy.start()
-    value_copy(v_hbm, 1, right).start()
-    value_copy(v_hbm, ring - 1, left).start()
+    for side in range(2):
+        for to, slot in ((right, 1), (left, ring - 1)):
+            key_copy(part_of(k_hbm, side), slot, side, to).start()
+        for to, slot in ((right, 1), (left, ring - 1)):
+            value_copy(part_of(v_hbm, side), slot, side, to).start()
+        if side == 0:
+            q_copy.start()
+
+    def tail_copies(src, dst, first_sem):
+        return [
+            remote(
+                src.at[pl.ds((side + 1) * half - edge, edge), :],
+                dst.at[tp, pl.ds(rows + side * edge, edge), :],
+                x_send.at[first_sem + side],
+                x_recv.at[first_sem + side],
+                to,
+            )
+            for side, to in enumerate((after, before))
+        ]
+
+    res_tails = tail_copies(res_hbm, res_all, 5)
+    for copy in res_tails:
+        copy.start()
+
+    def spread_each(which, buf, act):
+        def one(step, carry):
+            ref = buf.at[tp, rim, :]
+            peer = lax.rem(tp + step, n_tp)
+            act(remote(ref, ref, h_send.at[which, step], h_recv.at[which, step], {"tp": peer}))
+            return carry
+
+        lax.fori_loop(1, n_tp, one, 0)
 
     targets = {
         "y": {"tp": tp_at(0, 1, 0)},
@@ -355,11 +388,12 @@
         jnp.int32, (LANES, LANES), 1
     )
 
-    def to_column(line):
-        return jnp.sum(jnp.where(diagonal, line, 0.0), axis=1, keepdims=True)
+    def to_column(line, count=LANES):
+        return jnp.sum(jnp.where(diagonal[:count], line, 0.0), axis=1, keepdims=True)
 
     def to_line(column):
-        return jnp.sum(jnp.where(diagonal, column, 0.0), axis=0, keepdims=True)
+        picked = jnp.where(diagonal[: column.shape[0]], column, 0.0)
+        return jnp.sum(picked, axis=0, keepdims=True)
 
     def scale_win():
         def block(head, carry):
@@ -397,44 +431,71 @@
         7: ((wo_a, wo_b), ((-1, 0), (1, 0))),
     }
 
+    def share_residual_rim():
+        for copy in res_tails:
+            copy.wait_recv()
+        spread_each(0, res_all, lambda copy: copy.start())
+
     def extra(number):
         names, offsets = plan[number]
         steps(*names)
         prepare(*offsets)
+        if number == 2:
+            share_residual_rim()
         if number == 3:
             scale_win()
+        if number == 5:
+            spread_each(0, res_all, lambda copy: copy.wait_recv())
     unit(q_ref, acc_own, max_own, 0, [(k_ref[:half, :], v_ref[:half, :])], True)
     unit(q_ref, acc_own, max_own, half, [(k_ref[half:, :], v_ref[half:, :])], True)
     unit(q_ref, acc_own, max_own, half, [(k_ref[:half, :], v_ref[:half, :])])
 
+    def key_wait(slot, side):
+        key_copy(part_of(k_hbm, side), slot, side, right).wait_recv()
+
+    def value_wait(slot, side):
+        value_copy(part_of(v_hbm, side), slot, side, right).wait_recv()
+
+    def when(condition, act):
+        if isinstance(condition, bool):
+            if condition:
+                act()
+        else:
+            pl.when(condition)(act)
+
+    def pass_keys(step, side):
+        back = ring - step
+        key_wait(step, side)
+        key_copy(part_of(kbuf.at[step], side), step + 1, side, right).start()
+        key_wait(back, side)
+        when(
+            step < top - 1,
+            lambda: key_copy(part_of(kbuf.at[back], side), back - 1, side, left).start(),
+        )
+
+    def pass_values(step, side):
+        back = ring - step
+        value_wait(step, side)
+        when(
+            step < top - 1,
+            lambda: value_copy(part_of(vbuf.at[step], side), step + 1, side, right).start(),
+        )
+        value_wait(back, side)
+        value_copy(part_of(vbuf.at[back], side), back - 1, side, left).start()
+
+    def meet_partner():
+        q_copy.wait_recv()
+        first_units([(k_ref, v_ref)])
+        third_unit([(k_ref, v_ref)])
+
     def turn(step, carry):
         back = ring - step
-        key_copy(k_ref, step, right).wait_recv()
-        key_copy(kbuf.at[step], step + 1, right).start()
-        key_copy(k_ref, back, left).wait_recv()
-
-        @pl.when(step < top - 1)
-        def _():
-            key_copy(kbuf.at[back], back - 1, left).start()
-
-        @pl.when(step > 1)
-        def _():
-            late((step - 1, back + 1))
-
-        @pl.when(step == 1)
-        def _():
-            q_copy.wait_recv()
-            first_units([(k_ref, v_ref)])
-            third_unit([(k_ref, v_ref)])
-
-        value_copy(v_ref, step, right).wait_recv()
-
-        @pl.when(step < top - 1)
-        def _():
-            value_copy(vbuf.at[step], step + 1, right).start()
-
-        value_copy(v_ref, back, left).wait_recv()
-        value_copy(vbuf.at[back], back - 1, left).start()
+        pass_keys(step, 0)
+        pl.when(step > 1)(lambda: pass_keys(step - 1, 1))
+        pl.when(step > 2)(lambda: late((step - 2, back + 2)))
+        pl.when(step == 1)(meet_partner)
+        pass_values(step, 0)
+        pl.when(step > 1)(lambda: pass_values(step - 1, 1))
         early((step, back))
         for number in range(1, top):
             pl.when(step == number)(functools.partial(extra, number))
@@ -443,59 +504,78 @@
     lax.fori_loop(1, top, turn, 0)
     for number in range(top, 8):
         extra(number)
-    late((top - 1, top + 1))
-    key_copy(k_ref, top, right).wait_recv()
-    value_copy(v_ref, top, left).wait_recv()
-    far = [(kbuf.at[top], vbuf.at[top])]
-    blocks = first_units(far)
-    third_unit(far)
-
-    def settle(acc, top_ref):
-        total = acc[:, LANES:]
+    key_wait(top, 0)
+    pass_keys(top - 1, 1)
+    if top > 2:
+        late((top - 2, top + 2))
+    value_wait(top, 0)
+    pass_values(top - 1, 1)
+    far = [(kbuf.at[slot], vbuf.at[slot]) for slot in (top - 1, top + 1, top)]
+    blocks = first_units(far[2:])
+    pl.when(y_hi == 0)(lambda: third_unit(far))
+
+    def settle(acc, top_ref, side):
+        at = pl.ds(side * half, half)
+        total = acc[at, LANES:]
         seen = total > 0.0
         inverse = 1.0 / jnp.where(seen, total, 1.0)
-        level = jnp.where(seen, top_ref[...] * scale + jnp.log2(jnp.where(seen, total, 1.0)), LOW)
-        return acc[:, :LANES] * inverse, level
-
-    mean_par, level_par = settle(acc_par, max_par)
-    o_send[...] = mean_par.astype(BF16)
-    st_send[...] = jnp.zeros_like(st_send)
-    for g in range(rows // LANES):
-        block = level_par[g * LANES : (g + 1) * LANES, :]
-        st_send[g : g + 1, :] = to_line(block)
-    sides = (pl.ds(0, half), pl.ds(half, half))
-    st_copy = remote(st_send, st_recv, x_send.at[1], x_recv.at[1], across)
-    st_copy.start()
+        level = jnp.where(
+            seen, top_ref[at, :] * scale + jnp.log2(jnp.where(seen, total, 1.0)), LOW
+        )
+        return acc[at, :LANES] * inverse, level
+
+    st_copies = [
+        remote(st_send.at[n], st_recv.at[n], x_send.at[1 + n], x_recv.at[1 + n], across)
+        for n in range(2)
+    ]
     o_copies = [
-        remote(o_send.at[at, :], o_recv.at[at, :], x_send.at[2 + n], x_recv.at[2 + n], across)
-        for n, at in enumerate(sides)
+        remote(part_of(o_send, n), part_of(o_recv, n), x_send.at[3 + n], x_recv.at[3 + n], across)
+        for n in range(2)
     ]
-    for copy in o_copies:
-        copy.start()
+
+    def send_partial(side):
+        mean, level = settle(acc_par, max_par, side)
+        o_send[side * half : (side + 1) * half, :] = mean.astype(BF16)
+        o_copies[side].start()
+        st_send[side] = jnp.zeros((8, LANES), F32)
+        for g in range(half // LANES):
+            st_send[side, g : g + 1, :] = to_line(level[g * LANES : (g + 1) * LANES])
+        st_copies[side].start()
+
+    send_partial(0)
+    for slot in (top - 1, top + 1):
+        last_unit(kbuf.at[slot], vbuf.at[slot], slot)
+    prepare((-1, 1), (1, 1))
+    key_wait(top, 1)
+    value_wait(top, 1)
+    pl.when(y_hi == 1)(lambda: third_unit(far))
+    send_partial(1)
     unit(q_ref, acc_own, max_own, half, blocks)
     last_unit(kbuf.at[top], vbuf.at[top], top)
-    mean_own, level_own = settle(acc_own, max_own)
     steps(wo_b)
-    prepare((-1, 1), (1, 1), (2, 0), (2, 1))
+    prepare((2, 0), (2, 1))
     hid_acc[...] = res_all[tp].astype(F32)
-    st_copy.wait_recv()
+    sides = (pl.ds(0, half), pl.ds(half, half))
+    att_tails = tail_copies(att_all.at[tp], att_all, 7)
 
     def join(side):
+        mean_own, level_own = settle(acc_own, max_own, side)
+        st_copies[side].wait_recv()
         o_copies[side].wait_recv()
-        for g in range(side * half // LANES, (side + 1) * half // LANES):
-            at = slice(g * LANES, (g + 1) * LANES)
-            level_other = to_column(st_recv[g : g + 1, :])
-            here = level_own[at, :]
+        for g in range(half // LANES):
+            inner = slice(g * LANES, (g + 1) * LANES)
+            at = slice(side * half + g * LANES, side * half + (g + 1) * LANES)
+            level_other = to_column(st_recv[side, g : g + 1, :])
+            here = level_own[inner, :]
             most = jnp.maximum(here, level_other)
             w_own = jnp.exp2(here - most)
             w_other = jnp.exp2(level_other - most)
-            joined = (w_own * mean_own[at, :] + w_other * o_recv[at, :].astype(F32)) / (
+            joined = (w_own * mean_own[inner, :] + w_other * o_recv[at, :].astype(F32)) / (
                 w_own + w_other
             )
             att_all[tp, at, :] = joined.astype(BF16)
 
-    def project(side):
-        at = sides[side]
+    def project(at):
 
         def apply(chip):
             left_side = jnp.concatenate(
@@ -521,52 +601,65 @@
 
         lax.fori_loop(1, n_tp, one, 0)
 
+    lines_used = half // LANES
+
     def finish_hidden(side):
-        at = sides[side]
-        hidden = hid_acc[at, :].astype(BF16)
-        hid_ref[at, :] = hidden
-        wide = hidden.astype(F32)
-        column = jnp.sum(wide * wide, axis=1, keepdims=True)
         sq_all[tp, side] = jnp.zeros((8, LANES), F32)
-        for g in range(half // LANES):
-            sq_all[tp, side, g : g + 1, :] = to_line(column[g * LANES : (g + 1) * LANES])
+
+        def squares(first, count, line):
+            hidden = hid_acc[first : first + count, :].astype(BF16)
+            if first < rows:
+                hid_ref[first : first + count, :] = hidden
+            wide = hidden.astype(F32)
+            sq_all[tp, side, line : line + 1, :] = to_line(
+                jnp.sum(wide * wide, axis=1, keepdims=True)
+            )
+
+        for g in range(lines_used):
+            squares(side * half + g * LANES, LANES, g)
+        if side:
+            squares(rows, 2 * edge, lines_used)
         square_each(side, lambda copy: copy.start())
-
-    edge = 2 * RIM
-    rim_copies = [
-        remote(
-            str_ref.at[(side + 1) * half - edge : (side + 1) * half, :],
-            halo.at[side],
-            x_send.at[4 + side],
-            x_recv.at[4 + side],
-            to,
-        )
-        for side, to in enumerate((after, before))
-    ]
 
     def finish_streams(side):
         square_each(side, lambda copy: copy.wait_recv())
         lines = jnp.sum(sq_all[:, side], axis=0)
-        for g in range(half // LANES):
-            at = slice(side * half + g * LANES, side * half + (g + 1) * LANES)
-            mean_square = to_column(lines[g : g + 1, :]) / (n_tp * LANES)
-            streams = (str_acc[at, :] * lax.rsqrt(mean_square + 1e-6)).astype(BF16)
-            str_ref[at, :] = streams
-            ext[side, RIM + g * LANES : RIM + (g + 1) * LANES, :] = streams.astype(F32)
-        rim_copies[side].start()
-
-    out_a = gather(0, 0, att_place, half, project(0))
-    out_b = gather(0, 1, att_place, half, project(1))
+
+        def streams(first, count, line):
+            mean_square = to_column(lines[line : line + 1, :], count) / (n_tp * LANES)
+            scaled = str_acc[first : first + count, :] * lax.rsqrt(mean_square + 1e-6)
+            return scaled.astype(BF16).astype(F32)
+
+        for g in range(lines_used):
+            at = slice(RIM + g * LANES, RIM + (g + 1) * LANES)
+            ext[side, at, :] = streams(side * half + g * LANES, LANES, g)
+        if side:
+            outside = streams(rows, 2 * edge, lines_used)
+            ext[0, :RIM, :] = jnp.where(dev == 0, 0.0, outside[RIM:edge])
+            ext[1, :RIM, :] = jnp.where(
+                dev == n_ctx - 1, ext[0, half : half + RIM, :], outside[edge + RIM :]
+            )
+
+    out_a = gather(0, 0, att_place, half, project(sides[0]))
+    out_b = gather(0, 1, att_place, half, project(sides[1]))
     join(0)
     next(out_a)
+    att_tails[0].start()
     join(1)
     next(out_b)
-    steps(out_a, out_a, out_b, out_b, out_a, out_a, out_a, out_b, out_a, out_b, out_a)
+    att_tails[1].start()
+    steps(out_a, out_a, out_b)
+    for copy in att_tails:
+        copy.wait_recv()
+    spread_each(1, att_all, lambda copy: copy.start())
+    steps(out_b, out_a, out_a, out_a, out_b, out_a, out_b, out_a)
     finish_hidden(0)
+    spread_each(1, att_all, lambda copy: copy.wait_recv())
+    project_rim = project(rim)
+    for chip in range(n_tp // 2):
+        project_rim(chip)
     steps(out_b, out_b)
     finish_hidden(1)
-    finish_streams(0)
-    finish_streams(1)
 
     lane_group = lax.broadcasted_iota(jnp.int32, (FILTER_TAPS, LANES), 1) // GROUP
     filt = jnp.zeros((FILTER_TAPS, LANES), F32)
@@ -596,26 +689,24 @@
         out = featured(1, low, count) * response
         gated_ref[side * half + low : side * half + high, :] = out.astype(BF16)
 
+    finish_streams(0)
     convolve(0, edge, half)
-    convolve(1, edge, half)
-    rim_copies[0].wait_recv()
-    ext[0, :RIM, :] = jnp.where(dev == 0, 0.0, halo[0].astype(F32)[RIM:])
+    finish_streams(1)
     convolve(0, 0, edge)
-    rim_copies[1].wait_recv()
-    first_tail = str_ref[half - edge : half, :].astype(F32)[RIM:]
-    ext[1, :RIM, :] = jnp.where(dev == n_ctx - 1, first_tail, halo[1].astype(F32)[RIM:])
-    convolve(1, 0, edge)
-
+    convolve(1, 0, half)
     def drain(slot, carry):
-        key_copy(k_ref, slot, right).wait_send()
-        value_copy(v_ref, slot, right).wait_send()
+        for side in range(2):
+            key_copy(part_of(k_hbm, side), slot, side, right).wait_send()
+            value_copy(part_of(v_hbm, side), slot, side, right).wait_send()
         return carry
 
     lax.fori_loop(1, ring, drain, 0)
 
     for side in range(2):
         square_each(side, lambda copy: copy.wait_send())
-    for copy in [q_copy, st_copy] + o_copies + rim_copies:
+    spread_each(0, res_all, lambda copy: copy.wait_send())
+    spread_each(1, att_all, lambda copy: copy.wait_send())
+    for copy in [q_copy] + st_copies + o_copies + res_tails + att_tails:
         copy.wait_send()
     for move in moves:
         move().wait_send()
@@ -651,27 +742,27 @@
             pltpu.VMEM((rows, width), F32),
             pltpu.VMEM((rows, width), BF16),
             pltpu.VMEM((rows, width), BF16),
-            pltpu.VMEM((8, LANES), F32),
-            pltpu.VMEM((8, LANES), F32),
+            pltpu.VMEM((2, 8, LANES), F32),
+            pltpu.VMEM((2, 8, LANES), F32),
             pltpu.VMEM((n_tp * LANES, n_tp * LANES), BF16),
             pltpu.VMEM((n_tp * LANES, 3 * LANES), BF16),
             pltpu.VMEM((n_tp * LANES, 3 * LANES), BF16),
-            pltpu.VMEM((n_tp, rows, width), BF16),
-            pltpu.VMEM((n_tp, rows, width), BF16),
-            pltpu.VMEM((rows, LANES), F32),
-            pltpu.VMEM((rows, 3 * LANES), F32),
+            pltpu.VMEM((n_tp, rows + 4 * RIM, width), BF16),
+            pltpu.VMEM((n_tp, rows + 4 * RIM, width), BF16),
+            pltpu.VMEM((rows + 4 * RIM, LANES), F32),
+            pltpu.VMEM((rows + 4 * RIM, 3 * LANES), F32),
             pltpu.VMEM((n_tp, 2, 8, LANES), F32),
-            pltpu.VMEM((rows, 3 * LANES), BF16),
-            pltpu.VMEM((2, 2 * RIM, 3 * LANES), BF16),
             pltpu.VMEM((2, RIM + half, 3 * LANES), F32),
             pltpu.VMEM((RIM + half, LANES), F32),
             dma((11,)),
-            dma((ring,)),
-            dma((ring,)),
-            dma((ring,)),
-            dma((ring,)),
-            dma((6,)),
-            dma((6,)),
+            dma((ring, 2)),
+            dma((ring, 2)),
+            dma((ring, 2)),
+            dma((ring, 2)),
+            dma((9,)),
+            dma((9,)),
+            dma((2, n_tp)),
+            dma((2, n_tp)),
             dma((2, n_tp)),
             dma((2, n_tp)),
             dma((3, 2, 17)),

time: 95.3 us -> 96.8 us (1.016)
  Pallas kernels: 93.2 us -> 94.7 us
    pallas_call x1, Pallas kernels: 93.2 us -> 94.7 us  [local(): pl.pallas_call(functools.partial(kernel, ring), out_shape=(shape, shape),...]
where the time goes in v4:
time: 96.8 us; the launch traced here: 96.7 us
  Pallas kernels  94.7 us (98%)
  local copies, waits for them, and re-layouts  1.31 us (1%)
    pallas_call x1, Pallas kernels, local(): pl.pallas_call(functools.partial(kernel, ring), out_shape=(shape, shape),...  94.7 us

profile of v4, /device:TPU:1, one launch (start us, length us, event | category | flops | bytes accessed | tf_op | source)
XLA Modules:
  0.0 96.7 jit_solution(15727962030859185528)
XLA Ops:
  0.6 94.7 %shard_map.104 = (bf16[512,128]{1,0:T(8,128)(2,1)S(1)}, bf16[512,128]{1,0:T(8,128)(2,1)S(1)}) custom-call(bf16[512,128]{1,0:T(8,128)(2,1)} %q_hbm.1, bf16[512,128]{1,0:T(8,128)(2,1)} %k_hbm.1, bf16[512,128]{1,0:T(8,128)(2,1)} %v_hbm.1, bf16[512,128]{1,0:T(8,128)(2,1)} %res_hbm.1, bf16[128,2048]{1,0:T(8,128)(2,1)} %outp_hbm.1, f32[16,128]{1,0:T(8,128)} %bitcast.3, ...), custom_call_target="tpu_custom_call" | custom-call | flops 4000000000 | bytes 4000000 | tf_op jit(solution)/shard_map/pallas_call | solution.py:724
  95.4 0.7 copy.13
  96.0 0.7 copy.14

commit v5 on v4

--- a/solution.py
+++ b/solution.py
@@ -40,6 +40,9 @@
     filt_ref,
     kbuf,
     vbuf,
+    vt_own,
+    qt_own,
+    qt_par,
     qpar,
     acc_own,
     acc_par,
@@ -155,17 +158,23 @@
         return remote(src, dst, ks_sem.at[slot, side], kr_sem.at[slot, side], to)
 
     def value_copy(src, slot, side, to):
-        dst = part_of(vbuf.at[slot], side)
-        return remote(src, dst, vs_sem.at[slot, side], vr_sem.at[slot, side], to)
+        return remote(
+            src, vbuf.at[slot, side], vs_sem.at[slot, side], vr_sem.at[slot, side], to
+        )
+
+    def turned(ref, side):
+        return ref[side * half : (side + 1) * half, :].astype(F32).T.astype(BF16)
 
     q_copy = remote(q_hbm, qpar, x_send.at[0], x_recv.at[0], across)
     for side in range(2):
         for to, slot in ((right, 1), (left, ring - 1)):
             key_copy(part_of(k_hbm, side), slot, side, to).start()
-        for to, slot in ((right, 1), (left, ring - 1)):
-            value_copy(part_of(v_hbm, side), slot, side, to).start()
         if side == 0:
             q_copy.start()
+            loads[2].wait()
+        vt_own[side] = turned(v_ref, side)
+        for to, slot in ((right, 1), (left, ring - 1)):
+            value_copy(vt_own.at[side], slot, side, to).start()
 
     def tail_copies(src, dst, first_sem):
         return [
@@ -306,61 +315,52 @@
 
         return x_first() if side else y_first()
 
-    ones = jnp.ones((half, LANES), BF16)
-    tri = lax.broadcasted_iota(jnp.int32, (half, half), 0) >= lax.broadcasted_iota(
+    ones = jnp.ones((16, half), BF16)
+    tri = lax.broadcasted_iota(jnp.int32, (half, half), 0) <= lax.broadcasted_iota(
         jnp.int32, (half, half), 1
     )
 
-    def unit(queries, acc, top_ref, offset, blocks, masked=False):
-        at = pl.ds(offset, half)
-        rows_q = queries[at, :]
-        scores = [
-            lax.dot_general(rows_q, keys, (((1,), (1,)), ((), ())), preferred_element_type=F32)
-            for keys, _ in blocks
-        ]
+    def unit(queries, acc, top_ref, side, blocks, masked=False):
+        these = queries[side]
+        scores = [jnp.dot(keys, these, preferred_element_type=F32) for keys, _ in blocks]
         if masked:
             scores = [jnp.where(tri, block, LOW) for block in scores]
-        old = top_ref[at, :]
+        old = top_ref[side, 0:1, :]
         best = functools.reduce(jnp.maximum, scores)
-        new = jnp.maximum(old, jnp.max(best, axis=1, keepdims=True))
-        top_ref[at, :] = new
-        wide = jnp.concatenate([new] * (half // LANES), axis=1)
-        factor = jnp.exp2((old - new) * scale)
-        total = acc[at, :] * jnp.concatenate([factor, factor], axis=1)
+        new = jnp.maximum(old, jnp.max(best, axis=0, keepdims=True))
+        top_ref[side, 0:1, :] = new
+        total = acc[side] * jnp.exp2((old - new) * scale)
         for block, (_, values) in zip(scores, blocks):
-            weights = jnp.exp2((block - wide) * scale).astype(BF16)
+            weights = jnp.exp2((block - new) * scale).astype(BF16)
             total = total + jnp.dot(
-                weights, jnp.concatenate([values, ones], axis=1), preferred_element_type=F32
+                jnp.concatenate([values, ones], axis=0), weights, preferred_element_type=F32
             )
-        acc[at, :] = total
-
-    row_c = pl.multiple_of(y_hi * half, half)
-
-    def first_units(pairs):
-        blocks = [(keys[:half, :], values[:half, :]) for keys, values in pairs]
-        unit(qpar, acc_par, max_par, half, blocks)
-        return blocks
-
-    def third_unit(pairs):
-        at = pl.ds(row_c, half)
-        unit(qpar, acc_par, max_par, row_c, [(keys[at, :], values[at, :]) for keys, values in pairs])
-
-    def last_unit(keys, values, slot):
-        row_d = pl.multiple_of(jnp.where(slot <= z, 0, half), half)
-        at = pl.ds(row_d, half)
-        unit(q_ref, acc_own, max_own, row_d, [(keys[at, :], values[at, :])])
+        acc[side] = total
+
+    def own_block(side):
+        return (k_ref[side * half : (side + 1) * half, :], vt_own[side])
+
+    def block_at(slot, side):
+        return (kbuf[slot, pl.ds(pl.multiple_of(side * half, half), half), :], vbuf[slot, side])
+
+    def third_unit(slots):
+        unit(qt_par, acc_par, max_par, y_hi, [block_at(slot, y_hi) for slot in slots])
+
+    def last_unit(slot):
+        side = jnp.where(slot <= z, 0, 1)
+        unit(qt_own, acc_own, max_own, side, [block_at(slot, side)])
 
     def early(slots):
-        pairs = [(kbuf.at[slot], vbuf.at[slot]) for slot in slots]
-        blocks = first_units(pairs)
-        unit(q_ref, acc_own, max_own, half, blocks)
+        blocks = [block_at(slot, 0) for slot in slots]
+        unit(qt_par, acc_par, max_par, 1, blocks)
+        unit(qt_own, acc_own, max_own, 1, blocks)
 
     def late(slots):
-        third_unit([(kbuf.at[slot], vbuf.at[slot]) for slot in slots])
+        third_unit(slots)
         for slot in slots:
-            last_unit(kbuf.at[slot], vbuf.at[slot], slot)
-
-    for load in loads[:5]:
+            last_unit(slot)
+
+    for load in loads[:2] + loads[3:5]:
         load.wait()
 
     def res_place(chunk, first, count):
@@ -446,15 +446,17 @@
             scale_win()
         if number == 5:
             spread_each(0, res_all, lambda copy: copy.wait_recv())
-    unit(q_ref, acc_own, max_own, 0, [(k_ref[:half, :], v_ref[:half, :])], True)
-    unit(q_ref, acc_own, max_own, half, [(k_ref[half:, :], v_ref[half:, :])], True)
-    unit(q_ref, acc_own, max_own, half, [(k_ref[:half, :], v_ref[:half, :])])
+    for side in range(2):
+        qt_own[side] = turned(q_ref, side)
+    unit(qt_own, acc_own, max_own, 0, [own_block(0)], True)
+    unit(qt_own, acc_own, max_own, 1, [own_block(1)], True)
+    unit(qt_own, acc_own, max_own, 1, [own_block(0)])
 
     def key_wait(slot, side):
         key_copy(part_of(k_hbm, side), slot, side, right).wait_recv()
 
     def value_wait(slot, side):
-        value_copy(part_of(v_hbm, side), slot, side, right).wait_recv()
+        value_copy(vt_own.at[side], slot, side, right).wait_recv()
 
     def when(condition, act):
         if isinstance(condition, bool):
@@ -478,15 +480,18 @@
         value_wait(step, side)
         when(
             step < top - 1,
-            lambda: value_copy(part_of(vbuf.at[step], side), step + 1, side, right).start(),
+            lambda: value_copy(vbuf.at[step, side], step + 1, side, right).start(),
         )
         value_wait(back, side)
-        value_copy(part_of(vbuf.at[back], side), back - 1, side, left).start()
+        value_copy(vbuf.at[back, side], back - 1, side, left).start()
 
     def meet_partner():
         q_copy.wait_recv()
-        first_units([(k_ref, v_ref)])
-        third_unit([(k_ref, v_ref)])
+        for side in range(2):
+            qt_par[side] = turned(qpar, side)
+        unit(qt_par, acc_par, max_par, 1, [own_block(0)])
+        pl.when(y_hi == 0)(lambda: unit(qt_par, acc_par, max_par, 0, [own_block(0)]))
+        pl.when(y_hi == 1)(lambda: unit(qt_par, acc_par, max_par, 1, [own_block(1)]))
 
     def turn(step, carry):
         back = ring - step
@@ -510,48 +515,43 @@
         late((top - 2, top + 2))
     value_wait(top, 0)
     pass_values(top - 1, 1)
-    far = [(kbuf.at[slot], vbuf.at[slot]) for slot in (top - 1, top + 1, top)]
-    blocks = first_units(far[2:])
+    far = (top - 1, top + 1, top)
+    unit(qt_par, acc_par, max_par, 1, [block_at(top, 0)])
     pl.when(y_hi == 0)(lambda: third_unit(far))
 
     def settle(acc, top_ref, side):
-        at = pl.ds(side * half, half)
-        total = acc[at, LANES:]
+        total = acc[side, width : width + 1, :]
         seen = total > 0.0
-        inverse = 1.0 / jnp.where(seen, total, 1.0)
-        level = jnp.where(
-            seen, top_ref[at, :] * scale + jnp.log2(jnp.where(seen, total, 1.0)), LOW
-        )
-        return acc[at, :LANES] * inverse, level
+        held = jnp.where(seen, total, 1.0)
+        level = jnp.where(seen, top_ref[side, 0:1, :] * scale + jnp.log2(held), LOW)
+        return acc[side, :width, :] * (1.0 / held), level
 
     st_copies = [
         remote(st_send.at[n], st_recv.at[n], x_send.at[1 + n], x_recv.at[1 + n], across)
         for n in range(2)
     ]
     o_copies = [
-        remote(part_of(o_send, n), part_of(o_recv, n), x_send.at[3 + n], x_recv.at[3 + n], across)
+        remote(o_send.at[n], o_recv.at[n], x_send.at[3 + n], x_recv.at[3 + n], across)
         for n in range(2)
     ]
 
     def send_partial(side):
         mean, level = settle(acc_par, max_par, side)
-        o_send[side * half : (side + 1) * half, :] = mean.astype(BF16)
+        o_send[side] = mean.astype(BF16)
         o_copies[side].start()
-        st_send[side] = jnp.zeros((8, LANES), F32)
-        for g in range(half // LANES):
-            st_send[side, g : g + 1, :] = to_line(level[g * LANES : (g + 1) * LANES])
+        st_send[side] = jnp.broadcast_to(level, (8, half))
         st_copies[side].start()
 
     send_partial(0)
     for slot in (top - 1, top + 1):
-        last_unit(kbuf.at[slot], vbuf.at[slot], slot)
+        last_unit(slot)
     prepare((-1, 1), (1, 1))
     key_wait(top, 1)
     value_wait(top, 1)
     pl.when(y_hi == 1)(lambda: third_unit(far))
     send_partial(1)
-    unit(q_ref, acc_own, max_own, half, blocks)
-    last_unit(kbuf.at[top], vbuf.at[top], top)
+    unit(qt_own, acc_own, max_own, 1, [block_at(top, 0)])
+    last_unit(top)
     steps(wo_b)
     prepare((2, 0), (2, 1))
     hid_acc[...] = res_all[tp].astype(F32)
@@ -562,18 +562,13 @@
         mean_own, level_own = settle(acc_own, max_own, side)
         st_copies[side].wait_recv()
         o_copies[side].wait_recv()
-        for g in range(half // LANES):
-            inner = slice(g * LANES, (g + 1) * LANES)
-            at = slice(side * half + g * LANES, side * half + (g + 1) * LANES)
-            level_other = to_column(st_recv[side, g : g + 1, :])
-            here = level_own[inner, :]
-            most = jnp.maximum(here, level_other)
-            w_own = jnp.exp2(here - most)
-            w_other = jnp.exp2(level_other - most)
-            joined = (w_own * mean_own[inner, :] + w_other * o_recv[at, :].astype(F32)) / (
-                w_own + w_other
-            )
-            att_all[tp, at, :] = joined.astype(BF16)
+        level_other = st_recv[side, 0:1, :]
+        most = jnp.maximum(level_own, level_other)
+        w_own = jnp.exp2(level_own - most)
+        w_other = jnp.exp2(level_other - most)
+        share = 1.0 / (w_own + w_other)
+        joined = mean_own * (w_own * share) + o_recv[side].astype(F32) * (w_other * share)
+        att_all[tp, side * half : (side + 1) * half, :] = joined.T.astype(BF16)
 
     def project(at):
 
@@ -734,16 +729,19 @@
             pltpu.VMEM((FEAT_TAPS, 3, LANES), F32),
             pltpu.VMEM((FILTER_TAPS, LANES // GROUP), F32),
             pltpu.VMEM((ring, rows, width), BF16),
-            pltpu.VMEM((ring, rows, width), BF16),
+            pltpu.VMEM((ring, 2, width, half), BF16),
+            pltpu.VMEM((2, width, half), BF16),
+            pltpu.VMEM((2, width, half), BF16),
+            pltpu.VMEM((2, width, half), BF16),
             pltpu.VMEM((rows, width), BF16),
-            pltpu.VMEM((rows, 2 * width), F32),
-            pltpu.VMEM((rows, 2 * width), F32),
-            pltpu.VMEM((rows, width), F32),
-            pltpu.VMEM((rows, width), F32),
-            pltpu.VMEM((rows, width), BF16),
-            pltpu.VMEM((rows, width), BF16),
-            pltpu.VMEM((2, 8, LANES), F32),
-            pltpu.VMEM((2, 8, LANES), F32),
+            pltpu.VMEM((2, width + 16, half), F32),
+            pltpu.VMEM((2, width + 16, half), F32),
+            pltpu.VMEM((2, 8, half), F32),
+            pltpu.VMEM((2, 8, half), F32),
+            pltpu.VMEM((2, width, half), BF16),
+            pltpu.VMEM((2, width, half), BF16),
+            pltpu.VMEM((2, 8, half), F32),
+            pltpu.VMEM((2, 8, half), F32),
             pltpu.VMEM((n_tp * LANES, n_tp * LANES), BF16),
             pltpu.VMEM((n_tp * LANES, 3 * LANES), BF16),
             pltpu.VMEM((n_tp * LANES, 3 * LANES), BF16),

time: 96.8 us -> 96.7 us (level)
  no operation moved by 1% of the time
where the time goes in v5:
time: 96.7 us; the launch traced here: 96.6 us
  Pallas kernels  94.6 us (98%)
  local copies, waits for them, and re-layouts  1.31 us (1%)
    pallas_call x1, Pallas kernels, local(): pl.pallas_call(functools.partial(kernel, ring), out_shape=(shape, shape),...  94.6 us

profile of v5, /device:TPU:1, one launch (start us, length us, event | category | flops | bytes accessed | tf_op | source)
XLA Modules:
  0.0 96.6 jit_solution(5850533726596976042)
XLA Ops:
  0.6 94.6 %shard_map.104 = (bf16[512,128]{1,0:T(8,128)(2,1)S(1)}, bf16[512,128]{1,0:T(8,128)(2,1)S(1)}) custom-call(bf16[512,128]{1,0:T(8,128)(2,1)} %q_hbm.1, bf16[512,128]{1,0:T(8,128)(2,1)} %k_hbm.1, bf16[512,128]{1,0:T(8,128)(2,1)} %v_hbm.1, bf16[512,128]{1,0:T(8,128)(2,1)} %res_hbm.1, bf16[128,2048]{1,0:T(8,128)(2,1)} %outp_hbm.1, f32[16,128]{1,0:T(8,128)} %bitcast.3, ...), custom_call_target="tpu_custom_call" | custom-call | flops 4000000000 | bytes 4000000 | tf_op jit(solution)/shard_map/pallas_call | solution.py:719
  95.2 0.7 copy.13
  95.9 0.7 copy.14

commit v6 on v5

--- a/solution.py
+++ b/solution.py
@@ -99,6 +99,7 @@
     right = ctx_id(y_hi, lax.rem(z + 1, ring))
     left = ctx_id(y_hi, lax.rem(z + ring - 1, ring))
     across = ctx_id(1 - y_hi, z)
+    beside = {"ctx": (1 - y_hi) * ring + z, "tp": tp + 2 - 4 * y_lo}
     after = {"ctx": lax.rem(dev + 1, n_ctx)}
     before = {"ctx": lax.rem(dev + n_ctx - 1, n_ctx)}
 
@@ -110,7 +111,7 @@
         )
 
     barrier = pltpu.get_barrier_semaphore()
-    for other in (right, left, across, after, before):
+    for other in (right, left, across, beside, after, before):
         pl.semaphore_signal(barrier, inc=1, device_id=other, device_id_type=MESH)
 
     def greet(step, carry):
@@ -143,7 +144,7 @@
     for acc, top_ref in ((acc_own, max_own), (acc_par, max_par)):
         acc[...] = jnp.zeros_like(acc)
         top_ref[...] = jnp.full(top_ref.shape, LOW, F32)
-    pl.semaphore_wait(barrier, n_tp - 1 + 5)
+    pl.semaphore_wait(barrier, n_tp - 1 + 6)
 
     def remote(src, dst, send, recv, to):
         return pltpu.make_async_remote_copy(
@@ -203,13 +204,14 @@
 
     targets = {
         "y": {"tp": tp_at(0, 1, 0)},
+        "yy": beside,
         "xp": {"tp": tp_at(1, 0, 0)},
         "xm": {"tp": tp_at(-1, 0, 0)},
         "c": {"tp": tp_at(0, 0, 1)},
     }
     moves = []
 
-    def gather(which, side, place, span, consume):
+    def gather(which, side, place, span, consume, twin=False):
         whole = (side * span, span)
         head = (side * span, span // 2)
         tail = (side * span + span // 2, span // 2)
@@ -222,15 +224,21 @@
             )
 
         def go(dx, dy, to, part=whole):
+            if twin and to == "y" and part == whole:
+                go(dx, dy, "y", head)
+                go(dx, dy, "yy", tail)
+                return
             number = len(known)
             known[dx, dy, to] = (number, part)
             copy_of(dx, dy, 0, part, number, to).start()
             moves.append(lambda: copy_of(dx, dy, 0, part, number, to))
 
         def come(dx, dy, to):
+            if twin and to == "y":
+                come(dx, dy, "yy")
             number, part = known[dx, dy, to]
             sx = dx + {"xp": -1, "xm": 1}.get(to, 0)
-            sy = 1 - dy if to == "y" else dy
+            sy = 1 - dy if to in ("y", "yy") else dy
             copy_of(sx, sy, 1 if to == "c" else 0, part, number, to).wait_recv()
 
         def pair(dx, dy):
@@ -377,9 +385,9 @@
 
     res_a = gather(1, 0, res_place, half, nothing)
     res_b = gather(1, 1, res_place, half, nothing)
-    wo_a = gather(2, 0, wo_place, LANES // 2, nothing)
-    wo_b = gather(2, 1, wo_place, LANES // 2, nothing)
-    for stages in (res_a, res_b, wo_a, wo_b):
+    wo_a = gather(2, 0, wo_place, LANES // 2, nothing, True)
+    wo_b = gather(2, 1, wo_place, LANES // 2, nothing, True)
+    for stages in (res_a, res_b):
         next(stages)
     for load in loads[5:]:
         load.wait()
@@ -422,13 +430,13 @@
             next(stages)
 
     plan = {
-        1: ((res_a, res_a, res_b), ()),
-        2: ((wo_a, wo_a, wo_b, res_a, res_a, res_b), ()),
-        3: ((res_a, res_b), ()),
-        4: ((wo_b, wo_a, wo_a, res_a, res_b), ()),
-        5: ((wo_a, wo_b, res_a, res_b), ()),
-        6: ((wo_a, wo_b, res_b), ((0, 0), (0, 1))),
-        7: ((wo_a, wo_b), ((-1, 0), (1, 0))),
+        1: ((res_a, res_a, res_b, wo_a), ()),
+        2: ((res_a, res_a, res_b, res_b, wo_b), ()),
+        3: ((wo_a, wo_a, res_a, res_a, res_b), ()),
+        4: ((wo_b, wo_b, res_a, res_b, res_b), ()),
+        5: ((wo_a, wo_a), ((0, 0),)),
+        6: ((wo_a, wo_b), ((-1, 0), (1, 0))),
+        7: ((wo_a, wo_b, wo_b), ((0, 1), (-1, 1))),
     }
 
     def share_residual_rim():
@@ -444,7 +452,7 @@
             share_residual_rim()
         if number == 3:
             scale_win()
-        if number == 5:
+        if number == 4:
             spread_each(0, res_all, lambda copy: copy.wait_recv())
     for side in range(2):
         qt_own[side] = turned(q_ref, side)
@@ -545,15 +553,15 @@
     send_partial(0)
     for slot in (top - 1, top + 1):
         last_unit(slot)
-    prepare((-1, 1), (1, 1))
+    steps(wo_a, wo_b)
+    prepare((1, 1), (2, 0))
     key_wait(top, 1)
     value_wait(top, 1)
     pl.when(y_hi == 1)(lambda: third_unit(far))
     send_partial(1)
     unit(qt_own, acc_own, max_own, 1, [block_at(top, 0)])
     last_unit(top)
-    steps(wo_b)
-    prepare((2, 0), (2, 1))
+    prepare((2, 1),)
     hid_acc[...] = res_all[tp].astype(F32)
     sides = (pl.ds(0, half), pl.ds(half, half))
     att_tails = tail_copies(att_all.at[tp], att_all, 7)
@@ -763,8 +771,8 @@
             dma((2, n_tp)),
             dma((2, n_tp)),
             dma((2, n_tp)),
-            dma((3, 2, 17)),
-            dma((3, 2, 17)),
+            dma((3, 2, 20)),
+            dma((3, 2, 20)),
         ],
         compiler_params=pltpu.CompilerParams(
             collective_id=0, has_side_effects=True, vmem_limit_bytes=40 * 1024 * 1024

time: 96.7 us -> 94.4 us (0.976)
  Pallas kernels: 94.6 us -> 92.3 us
    pallas_call x1, Pallas kernels: 94.6 us -> 92.3 us  [local(): pl.pallas_call(functools.partial(kernel, ring), out_shape=(shape, shape),...]
where the time goes in v6:
time: 94.4 us; the launch traced here: 94.2 us
  Pallas kernels  92.3 us (98%)
  local copies, waits for them, and re-layouts  1.31 us (1%)
    pallas_call x1, Pallas kernels, local(): pl.pallas_call(functools.partial(kernel, ring), out_shape=(shape, shape),...  92.3 us

profile of v6, /device:TPU:1, one launch (start us, length us, event | category | flops | bytes accessed | tf_op | source)
XLA Modules:
  0.0 94.2 jit_solution(927352125287988072)
XLA Ops:
  0.6 92.3 %shard_map.104 = (bf16[512,128]{1,0:T(8,128)(2,1)S(1)}, bf16[512,128]{1,0:T(8,128)(2,1)S(1)}) custom-call(bf16[512,128]{1,0:T(8,128)(2,1)} %q_hbm.1, bf16[512,128]{1,0:T(8,128)(2,1)} %k_hbm.1, bf16[512,128]{1,0:T(8,128)(2,1)} %v_hbm.1, bf16[512,128]{1,0:T(8,128)(2,1)} %res_hbm.1, bf16[128,2048]{1,0:T(8,128)(2,1)} %outp_hbm.1, f32[16,128]{1,0:T(8,128)} %bitcast.3, ...), custom_call_target="tpu_custom_call" | custom-call | flops 4000000000 | bytes 4000000 | tf_op jit(solution)/shard_map/pallas_call | solution.py:727
  92.9 0.7 copy.13
  93.6 0.7 copy.14

commit v7 on v6

--- a/solution.py
+++ b/solution.py
@@ -309,8 +309,8 @@
             go(-1, 1, "c")
             come(1, 0, "y")
             go(1, 1, "c")
-            yield
             pair(0, 1)
+            yield
             pair(2, 0)
             yield
             come(2, 0, "y")
@@ -321,7 +321,7 @@
             pair(2, 1)
             yield
 
-        return x_first() if side else y_first()
+        return x_first() if side % 2 else y_first()
 
     ones = jnp.ones((16, half), BF16)
     tri = lax.broadcasted_iota(jnp.int32, (half, half), 0) <= lax.broadcasted_iota(
@@ -387,7 +387,7 @@
     res_b = gather(1, 1, res_place, half, nothing)
     wo_a = gather(2, 0, wo_place, LANES // 2, nothing, True)
     wo_b = gather(2, 1, wo_place, LANES // 2, nothing, True)
-    for stages in (res_a, res_b):
+    for stages in (res_a, res_b, wo_a):
         next(stages)
     for load in loads[5:]:
         load.wait()
@@ -430,13 +430,13 @@
             next(stages)
 
     plan = {
-        1: ((res_a, res_a, res_b, wo_a), ()),
-        2: ((res_a, res_a, res_b, res_b, wo_b), ()),
-        3: ((wo_a, wo_a, res_a, res_a, res_b), ()),
-        4: ((wo_b, wo_b, res_a, res_b, res_b), ()),
-        5: ((wo_a, wo_a), ((0, 0),)),
-        6: ((wo_a, wo_b), ((-1, 0), (1, 0))),
-        7: ((wo_a, wo_b, wo_b), ((0, 1), (-1, 1))),
+        1: ((), ()),
+        2: ((res_a, res_a, res_b, wo_b), ()),
+        3: ((wo_a, wo_a, res_a, res_b), ()),
+        4: ((wo_b, wo_b, res_a, res_b), ()),
+        5: ((wo_a, wo_a, res_a, res_b), ((0, 0),)),
+        6: ((wo_a, res_a, res_b), ((-1, 0),)),
+        7: ((wo_a, wo_b, res_a, res_b), ((1, 0), (0, 1))),
     }
 
     def share_residual_rim():
@@ -526,6 +526,7 @@
     far = (top - 1, top + 1, top)
     unit(qt_par, acc_par, max_par, 1, [block_at(top, 0)])
     pl.when(y_hi == 0)(lambda: third_unit(far))
+    pl.when(y_hi == 1)(lambda: third_unit(far[:2]))
 
     def settle(acc, top_ref, side):
         total = acc[side, width : width + 1, :]
@@ -553,15 +554,16 @@
     send_partial(0)
     for slot in (top - 1, top + 1):
         last_unit(slot)
-    steps(wo_a, wo_b)
-    prepare((1, 1), (2, 0))
+    steps(wo_a, wo_b, wo_b)
+    prepare((-1, 1), (1, 1))
     key_wait(top, 1)
     value_wait(top, 1)
-    pl.when(y_hi == 1)(lambda: third_unit(far))
+    pl.when(y_hi == 1)(lambda: third_unit(far[2:]))
     send_partial(1)
     unit(qt_own, acc_own, max_own, 1, [block_at(top, 0)])
     last_unit(top)
-    prepare((2, 1),)
+    steps(wo_b)
+    prepare((2, 0), (2, 1))
     hid_acc[...] = res_all[tp].astype(F32)
     sides = (pl.ds(0, half), pl.ds(half, half))
     att_tails = tail_copies(att_all.at[tp], att_all, 7)
@@ -643,25 +645,34 @@
                 dev == n_ctx - 1, ext[0, half : half + RIM, :], outside[edge + RIM :]
             )
 
-    out_a = gather(0, 0, att_place, half, project(sides[0]))
-    out_b = gather(0, 1, att_place, half, project(sides[1]))
+    outs = [
+        gather(0, n, att_place, half // 2, project(pl.ds(n * half // 2, half // 2)))
+        for n in range(4)
+    ]
+
+    def advance(first, *which):
+        steps(*(outs[first + n] for n in which))
+
     join(0)
-    next(out_a)
+    advance(0, 0, 1)
     att_tails[0].start()
     join(1)
-    next(out_b)
+    advance(2, 0, 1)
     att_tails[1].start()
-    steps(out_a, out_a, out_b)
+    advance(0, 0, 0, 1, 1)
+    advance(2, 0, 0, 1, 1)
     for copy in att_tails:
         copy.wait_recv()
     spread_each(1, att_all, lambda copy: copy.start())
-    steps(out_b, out_a, out_a, out_a, out_b, out_a, out_b, out_a)
+    advance(0, 0, 0, 0, 1)
+    advance(2, 0, 0, 0, 1)
+    advance(0, 0, 1, 0, 1, 1)
     finish_hidden(0)
     spread_each(1, att_all, lambda copy: copy.wait_recv())
     project_rim = project(rim)
     for chip in range(n_tp // 2):
         project_rim(chip)
-    steps(out_b, out_b)
+    advance(2, 0, 1, 0, 1, 1)
     finish_hidden(1)
 
     lane_group = lax.broadcasted_iota(jnp.int32, (FILTER_TAPS, LANES), 1) // GROUP
@@ -771,8 +782,8 @@
             dma((2, n_tp)),
             dma((2, n_tp)),
             dma((2, n_tp)),
-            dma((3, 2, 20)),
-            dma((3, 2, 20)),
+            dma((3, 4, 20)),
+            dma((3, 4, 20)),
         ],
         compiler_params=pltpu.CompilerParams(
             collective_id=0, has_side_effects=True, vmem_limit_bytes=40 * 1024 * 1024

time: 94.4 us -> 96.6 us (1.023)
  Pallas kernels: 92.3 us -> 94.5 us
    pallas_call x1, Pallas kernels: 92.3 us -> 94.5 us  [local(): pl.pallas_call(functools.partial(kernel, ring), out_shape=(shape, shape),...]
where the time goes in v7:
time: 96.6 us; the launch traced here: 96.5 us
  Pallas kernels  94.5 us (98%)
  local copies, waits for them, and re-layouts  1.31 us (1%)
    pallas_call x1, Pallas kernels, local(): pl.pallas_call(functools.partial(kernel, ring), out_shape=(shape, shape),...  94.5 us

profile of v7, /device:TPU:1, one launch (start us, length us, event | category | flops | bytes accessed | tf_op | source)
XLA Modules:
  0.0 96.5 jit_solution(15675239726020693044)
XLA Ops:
  0.6 94.5 %shard_map.104 = (bf16[512,128]{1,0:T(8,128)(2,1)S(1)}, bf16[512,128]{1,0:T(8,128)(2,1)S(1)}) custom-call(bf16[512,128]{1,0:T(8,128)(2,1)} %q_hbm.1, bf16[512,128]{1,0:T(8,128)(2,1)} %k_hbm.1, bf16[512,128]{1,0:T(8,128)(2,1)} %v_hbm.1, bf16[512,128]{1,0:T(8,128)(2,1)} %res_hbm.1, bf16[128,2048]{1,0:T(8,128)(2,1)} %outp_hbm.1, f32[16,128]{1,0:T(8,128)} %bitcast.3, ...), custom_call_target="tpu_custom_call" | custom-call | flops 4000000000 | bytes 4000000 | tf_op jit(solution)/shard_map/pallas_call | solution.py:738
  95.2 0.7 copy.13
  95.8 0.7 copy.14

commit v8 on v6

--- a/solution.py
+++ b/solution.py
@@ -151,31 +151,24 @@
             src_ref=src, dst_ref=dst, send_sem=send, recv_sem=recv, device_id=to, device_id_type=MESH
         )
 
-    def part_of(ref, side):
-        return ref.at[pl.ds(side * half, half), :]
-
-    def key_copy(src, slot, side, to):
-        dst = part_of(kbuf.at[slot], side)
-        return remote(src, dst, ks_sem.at[slot, side], kr_sem.at[slot, side], to)
-
-    def value_copy(src, slot, side, to):
-        return remote(
-            src, vbuf.at[slot, side], vs_sem.at[slot, side], vr_sem.at[slot, side], to
-        )
+    def key_copy(src, slot, to):
+        return remote(src, kbuf.at[slot], ks_sem.at[slot], kr_sem.at[slot], to)
+
+    def value_copy(src, slot, to):
+        return remote(src, vbuf.at[slot], vs_sem.at[slot], vr_sem.at[slot], to)
 
     def turned(ref, side):
         return ref[side * half : (side + 1) * half, :].astype(F32).T.astype(BF16)
 
     q_copy = remote(q_hbm, qpar, x_send.at[0], x_recv.at[0], across)
+    key_copy(k_hbm, 1, right).start()
+    key_copy(k_hbm, ring - 1, left).start()
+    q_copy.start()
+    loads[2].wait()
     for side in range(2):
-        for to, slot in ((right, 1), (left, ring - 1)):
-            key_copy(part_of(k_hbm, side), slot, side, to).start()
-        if side == 0:
-            q_copy.start()
-            loads[2].wait()
         vt_own[side] = turned(v_ref, side)
-        for to, slot in ((right, 1), (left, ring - 1)):
-            value_copy(vt_own.at[side], slot, side, to).start()
+    value_copy(vt_own, 1, right).start()
+    value_copy(vt_own, ring - 1, left).start()
 
     def tail_copies(src, dst, first_sem):
         return [
@@ -460,38 +453,32 @@
     unit(qt_own, acc_own, max_own, 1, [own_block(1)], True)
     unit(qt_own, acc_own, max_own, 1, [own_block(0)])
 
-    def key_wait(slot, side):
-        key_copy(part_of(k_hbm, side), slot, side, right).wait_recv()
-
-    def value_wait(slot, side):
-        value_copy(vt_own.at[side], slot, side, right).wait_recv()
-
-    def when(condition, act):
-        if isinstance(condition, bool):
-            if condition:
-                act()
-        else:
-            pl.when(condition)(act)
-
-    def pass_keys(step, side):
+    def key_wait(slot):
+        key_copy(k_hbm, slot, right).wait_recv()
+
+    def value_wait(slot):
+        value_copy(vt_own, slot, right).wait_recv()
+
+    def pass_keys(step):
         back = ring - step
-        key_wait(step, side)
-        key_copy(part_of(kbuf.at[step], side), step + 1, side, right).start()
-        key_wait(back, side)
-        when(
-            step < top - 1,
-            lambda: key_copy(part_of(kbuf.at[back], side), back - 1, side, left).start(),
-        )
-
-    def pass_values(step, side):
+        key_wait(step)
+        key_copy(kbuf.at[step], step + 1, right).start()
+        key_wait(back)
+
+        @pl.when(step < top - 1)
+        def _():
+            key_copy(kbuf.at[back], back - 1, left).start()
+
+    def pass_values(step):
         back = ring - step
-        value_wait(step, side)
-        when(
-            step < top - 1,
-            lambda: value_copy(vbuf.at[step, side], step + 1, side, right).start(),
-        )
-        value_wait(back, side)
-        value_copy(vbuf.at[back, side], back - 1, side, left).start()
+        value_wait(step)
+
+        @pl.when(step < top - 1)
+        def _():
+            value_copy(vbuf.at[step], step + 1, right).start()
+
+        value_wait(back)
+        value_copy(vbuf.at[back], back - 1, left).start()
 
     def meet_partner():
         q_copy.wait_recv()
@@ -503,12 +490,10 @@
 
     def turn(step, carry):
         back = ring - step
-        pass_keys(step, 0)
-        pl.when(step > 1)(lambda: pass_keys(step - 1, 1))
-        pl.when(step > 2)(lambda: late((step - 2, back + 2)))
+        pass_keys(step)
+        pl.when(step > 1)(lambda: late((step - 1, back + 1)))
         pl.when(step == 1)(meet_partner)
-        pass_values(step, 0)
-        pl.when(step > 1)(lambda: pass_values(step - 1, 1))
+        pass_values(step)
         early((step, back))
         for number in range(1, top):
             pl.when(step == number)(functools.partial(extra, number))
@@ -517,15 +502,12 @@
     lax.fori_loop(1, top, turn, 0)
     for number in range(top, 8):
         extra(number)
-    key_wait(top, 0)
-    pass_keys(top - 1, 1)
-    if top > 2:
-        late((top - 2, top + 2))
-    value_wait(top, 0)
-    pass_values(top - 1, 1)
-    far = (top - 1, top + 1, top)
+    late((top - 1, top + 1))
+    prepare((1, 1), (2, 0))
+    key_wait(top)
+    value_wait(top)
     unit(qt_par, acc_par, max_par, 1, [block_at(top, 0)])
-    pl.when(y_hi == 0)(lambda: third_unit(far))
+    third_unit((top,))
 
     def settle(acc, top_ref, side):
         total = acc[side, width : width + 1, :]
@@ -551,17 +533,11 @@
         st_copies[side].start()
 
     send_partial(0)
-    for slot in (top - 1, top + 1):
-        last_unit(slot)
-    steps(wo_a, wo_b)
-    prepare((1, 1), (2, 0))
-    key_wait(top, 1)
-    value_wait(top, 1)
-    pl.when(y_hi == 1)(lambda: third_unit(far))
     send_partial(1)
     unit(qt_own, acc_own, max_own, 1, [block_at(top, 0)])
     last_unit(top)
-    prepare((2, 1),)
+    steps(wo_a, wo_b)
+    prepare((2, 1))
     hid_acc[...] = res_all[tp].astype(F32)
     sides = (pl.ds(0, half), pl.ds(half, half))
     att_tails = tail_copies(att_all.at[tp], att_all, 7)
@@ -698,9 +674,8 @@
     convolve(0, 0, edge)
     convolve(1, 0, half)
     def drain(slot, carry):
-        for side in range(2):
-            key_copy(part_of(k_hbm, side), slot, side, right).wait_send()
-            value_copy(part_of(v_hbm, side), slot, side, right).wait_send()
+        key_copy(k_hbm, slot, right).wait_send()
+        value_copy(vt_own, slot, right).wait_send()
         return carry
 
     lax.fori_loop(1, ring, drain, 0)
@@ -761,10 +736,10 @@
             pltpu.VMEM((2, RIM + half, 3 * LANES), F32),
             pltpu.VMEM((RIM + half, LANES), F32),
             dma((11,)),
-            dma((ring, 2)),
-            dma((ring, 2)),
-            dma((ring, 2)),
-            dma((ring, 2)),
+            dma((ring,)),
+            dma((ring,)),
+            dma((ring,)),
+            dma((ring,)),
             dma((9,)),
             dma((9,)),
             dma((2, n_tp)),

time: 94.4 us -> 93.8 us (level)
  no operation moved by 1% of the time
where the time goes in v8:
time: 93.8 us; the launch traced here: 93.7 us
  Pallas kernels  91.7 us (98%)
  local copies, waits for them, and re-layouts  1.31 us (1%)
    pallas_call x1, Pallas kernels, local(): pl.pallas_call(functools.partial(kernel, ring), out_shape=(shape, shape),...  91.7 us

profile of v8, /device:TPU:1, one launch (start us, length us, event | category | flops | bytes accessed | tf_op | source)
XLA Modules:
  0.0 93.7 jit_solution(15212135463642853340)
XLA Ops:
  0.6 91.7 %shard_map.104 = (bf16[512,128]{1,0:T(8,128)(2,1)S(1)}, bf16[512,128]{1,0:T(8,128)(2,1)S(1)}) custom-call(bf16[512,128]{1,0:T(8,128)(2,1)} %q_hbm.1, bf16[512,128]{1,0:T(8,128)(2,1)} %k_hbm.1, bf16[512,128]{1,0:T(8,128)(2,1)} %v_hbm.1, bf16[512,128]{1,0:T(8,128)(2,1)} %res_hbm.1, bf16[128,2048]{1,0:T(8,128)(2,1)} %outp_hbm.1, f32[16,128]{1,0:T(8,128)} %bitcast.3, ...), custom_call_target="tpu_custom_call" | custom-call | flops 4000000000 | bytes 4000000 | tf_op jit(solution)/shard_map/pallas_call | solution.py:702
  92.3 0.7 copy.13
  93.0 0.7 copy.14

commit v9 on v8

--- a/solution.py
+++ b/solution.py
@@ -568,14 +568,14 @@
 
         return apply
 
-    def square_copy(side, step):
+    def square_copy(step):
         peer = lax.rem(tp + step, n_tp)
-        ref = sq_all.at[tp, side]
-        return remote(ref, ref, w_send.at[side, step], w_recv.at[side, step], {"tp": peer})
-
-    def square_each(side, act):
+        ref = sq_all.at[tp]
+        return remote(ref, ref, w_send.at[step], w_recv.at[step], {"tp": peer})
+
+    def square_each(act):
         def one(step, carry):
-            act(square_copy(side, step))
+            act(square_copy(step))
             return carry
 
         lax.fori_loop(1, n_tp, one, 0)
@@ -598,10 +598,9 @@
             squares(side * half + g * LANES, LANES, g)
         if side:
             squares(rows, 2 * edge, lines_used)
-        square_each(side, lambda copy: copy.start())
+            square_each(lambda copy: copy.start())
 
     def finish_streams(side):
-        square_each(side, lambda copy: copy.wait_recv())
         lines = jnp.sum(sq_all[:, side], axis=0)
 
         def streams(first, count, line):
@@ -668,6 +667,7 @@
         out = featured(1, low, count) * response
         gated_ref[side * half + low : side * half + high, :] = out.astype(BF16)
 
+    square_each(lambda copy: copy.wait_recv())
     finish_streams(0)
     convolve(0, edge, half)
     finish_streams(1)
@@ -680,8 +680,7 @@
 
     lax.fori_loop(1, ring, drain, 0)
 
-    for side in range(2):
-        square_each(side, lambda copy: copy.wait_send())
+    square_each(lambda copy: copy.wait_send())
     spread_each(0, res_all, lambda copy: copy.wait_send())
     spread_each(1, att_all, lambda copy: copy.wait_send())
     for copy in [q_copy] + st_copies + o_copies + res_tails + att_tails:
@@ -742,8 +741,8 @@
             dma((ring,)),
             dma((9,)),
             dma((9,)),
-            dma((2, n_tp)),
-            dma((2, n_tp)),
+            dma((n_tp,)),
+            dma((n_tp,)),
             dma((2, n_tp)),
             dma((2, n_tp)),
             dma((3, 2, 20)),

time: 93.8 us -> 93.8 us (level)
  no operation moved by 1% of the time
where the time goes in v9:
time: 93.8 us; the launch traced here: 93.7 us
  Pallas kernels  91.7 us (98%)
  local copies, waits for them, and re-layouts  1.31 us (1%)
    pallas_call x1, Pallas kernels, local(): pl.pallas_call(functools.partial(kernel, ring), out_shape=(shape, shape),...  91.7 us

profile of v9, /device:TPU:1, one launch (start us, length us, event | category | flops | bytes accessed | tf_op | source)
XLA Modules:
  0.0 93.7 jit_solution(12368825139988461386)
XLA Ops:
  0.6 91.7 %shard_map.104 = (bf16[512,128]{1,0:T(8,128)(2,1)S(1)}, bf16[512,128]{1,0:T(8,128)(2,1)S(1)}) custom-call(bf16[512,128]{1,0:T(8,128)(2,1)} %q_hbm.1, bf16[512,128]{1,0:T(8,128)(2,1)} %k_hbm.1, bf16[512,128]{1,0:T(8,128)(2,1)} %v_hbm.1, bf16[512,128]{1,0:T(8,128)(2,1)} %res_hbm.1, bf16[128,2048]{1,0:T(8,128)(2,1)} %outp_hbm.1, f32[16,128]{1,0:T(8,128)} %bitcast.3, ...), custom_call_target="tpu_custom_call" | custom-call | flops 4000000000 | bytes 4000000 | tf_op jit(solution)/shard_map/pallas_call | solution.py:701
  92.4 0.7 copy.13
  93.0 0.7 copy.14
